TPU v7x, 512 devices: a whole 4x8x8 slice. The times are simulated.
512 devices in a mesh: leaf: 64 (over x, y, core), grid: 8 (over z).
Axes of the slice: x: 4, y: 8, z: 8, core: 2. Of those that a mesh axis runs over, the one named last changes fastest.
Arguments:
- right_side: float32 [7, 256, 4096], P(None, None, ('leaf', 'grid')), may hold values from -6 to 6
- diag_inv: float32 [4096, 8128], P('leaf'), as said below
- off_diag: float32 [21, 256, 4096], P(None, None, 'leaf'), may hold values from -0.09375 to 0.09375
- tile_rows: int32 [21, 2, 64], P(None, None, 'leaf'), may hold values from 0 to 31, as said below
Outputs:
- forward_solution: float32 [7, 256, 4096], P(None, None, ('leaf', 'grid'))
- solution: float32 [7, 256, 4096], P(None, None, ('leaf', 'grid'))
Inputs may be any that keep to these rules, and one draw needn't show every extreme that they name: tile_rows[p, t, i] for the pair p of levels l < k names one of the 64 * 2^k / 128 tiles of 128 rows of the level-k separator above leaf index i. Within each separator's block of diag_inv, the diagonal entries lie near 0.8 to 1.2, and every row's other entries have a root mean square of about 0.5 divided by the square root of the separator's width.
All inputs are finite; a program needn't handle non-finite values.
Results may differ from a plain program's by a relative error of at most 0.0001.
Values sent between devices are 32-bit elements; how exact they have to be, the bound alone decides.
A program may use at most 64 MiB of HBM per device.

v0:
```python
import jax
import jax.numpy as jnp
from jax import lax
from jax.sharding import PartitionSpec as P

TILE = 128


highest = lax.Precision.HIGHEST


def from_partner(block, axis, apart):
    count = lax.axis_size(axis)
    route = []
    for low in range(count):
        high = low | 1 << apart
        if high != low and high < count:
            route += [(low, high), (high, low)]
    return lax.ppermute(block, axis, route)


def pair_slot(source, ancestor):
    return ancestor * (ancestor - 1) // 2 + source


def contract_last(left, right):
    return lax.dot_general(
        left, right, (((1,), (1,)), ((), ())), precision=highest, preferred_element_type=jnp.float32
    )


def local(right_side, diag_inv, off_diag, tile_rows):
    depth_count = right_side.shape[0]
    rows_dev = diag_inv.shape[0]
    tile_count = off_diag.shape[1] // TILE
    leaf_index = lax.axis_index("leaf")
    local_side = lax.all_to_all(right_side, "grid", split_axis=1, concat_axis=2, tiled=True)
    rhs_dev = local_side.shape[1]
    forward_rows = []
    for height in range(depth_count):
        node_width = rows_dev * 2**height
        offset = rows_dev * (2**height - 1)
        position = leaf_index % 2**height * rows_dev
        partial_value = jnp.zeros((rhs_dev, node_width), jnp.float32)
        partial_value = lax.dynamic_update_slice(partial_value, local_side[height], (0, position))
        for source in range(height):
            pair = pair_slot(source, height)
            addend = contract_last(forward_rows[source], off_diag[pair])
            for tile_number in range(tile_count):
                column = tile_rows[pair, tile_number, 0] * TILE
                current = lax.dynamic_slice(partial_value, (0, column), (rhs_dev, TILE))
                piece = addend[:, tile_number * TILE : (tile_number + 1) * TILE]
                partial_value = lax.dynamic_update_slice(
                    partial_value, current - piece, (0, column)
                )
        if height > 0:
            for bit_number in range(height):
                partial_value = partial_value + from_partner(partial_value, "leaf", bit_number)
        forward_rows.append(contract_last(partial_value, diag_inv[:, offset : offset + node_width]))
    full_solution = [None] * depth_count
    local_solution = [None] * depth_count
    for height in reversed(range(depth_count)):
        node_width = rows_dev * 2**height
        offset = rows_dev * (2**height - 1)
        position = leaf_index % 2**height * rows_dev
        known_part = jnp.zeros((rhs_dev, rows_dev), jnp.float32)
        for ancestor in range(height + 1, depth_count):
            pair = pair_slot(height, ancestor)
            pieces = []
            for tile_number in range(tile_count):
                column = tile_rows[pair, tile_number, 0] * TILE
                pieces.append(
                    lax.dynamic_slice(full_solution[ancestor], (0, column), (rhs_dev, TILE))
                )
            picked = jnp.concatenate(pieces, axis=1)
            known_part = known_part + jnp.dot(
                picked, off_diag[pair], precision=highest, preferred_element_type=jnp.float32
            )
        residue = forward_rows[height] - known_part
        partial_value = jnp.dot(
            residue,
            diag_inv[:, offset : offset + node_width],
            precision=highest,
            preferred_element_type=jnp.float32,
        )
        if height > 0:
            for bit_number in range(height):
                partial_value = partial_value + from_partner(partial_value, "leaf", bit_number)
        full_solution[height] = partial_value
        local_solution[height] = lax.dynamic_slice_in_dim(partial_value, position, rows_dev, 1)
    forward_out, solution_out = (
        lax.all_to_all(jnp.stack(forward_rows), "grid", split_axis=2, concat_axis=1, tiled=True),
        lax.all_to_all(jnp.stack(local_solution), "grid", split_axis=2, concat_axis=1, tiled=True),
    )
    return (forward_out, solution_out)


def solution(mesh):
    in_specs = (
        P(None, None, ("leaf", "grid")),
        P("leaf", None),
        P(None, None, "leaf"),
        P(None, None, "leaf"),
    )
    out_specs = (P(None, None, ("leaf", "grid")), P(None, None, ("leaf", "grid")))
    return jax.shard_map(local, mesh=mesh, in_specs=in_specs, out_specs=out_specs, check_vma=False)
```

profile of v0, /device:TPU:1, one launch (start us, length us, event | category | flops | bytes accessed | tf_op | source)
XLA Modules:
  0.0 614.8 jit_solution(13524185497446127236)
XLA Ops:
  2.9 10.9 %all-to-all-start = ((f32[8,1,1792]{2,1,0:T(1,128)}), f32[8,1,1792]{2,1,0:T(1,128)S(1)}, u32[]{:S(2)}, u32[]{:S(2)}) async-start(f32[8,1,1792]{2,1,0:T(1,128)} %reshape.98), calls=%async_computation | async-start | bytes 114688 | tf_op jit(solution)/shard_map/all_to_all | solution.py:37
  153.3 7.8 %collective-permute-start.9 = (f32[32,1024]{1,0:T(8,128)S(1)}, f32[32,1024]{1,0:T(8,128)S(1)}, u32[]{:S(2)}, u32[]{:S(2)}) collective-permute-start(f32[32,1024]{1,0:T(8,128)S(1)} %add.464), channel_id=1, source_target_pairs={{0,64},{64,0},{8,72},{72,8},{16,80},{80,16},{24,88},{88,24},{32,96... | collective-permute-start | bytes 393224 | tf_op jit(solution)/shard_map/ppermute | solution.py:19
  167.9 6.2 %collective-permute-start.10 = (f32[32,2048]{1,0:T(8,128)}, f32[32,2048]{1,0:T(8,128)S(1)}, u32[]{:S(2)}, u32[]{:S(2)}) collective-permute-start(f32[32,2048]{1,0:T(8,128)} %constant_dynamic-update-slice_fusion.12), channel_id=1, source_target_pairs={{0,8},{8,0},{16,24},{24,16},{32,40},{40,32},{48,56},{56,48},{64,72... | collective-permute-start | bytes 786440 | tf_op jit(solution)/shard_map/ppermute | solution.py:19
  178.4 7.4 %collective-permute-done.11 = f32[32,2048]{1,0:T(8,128)S(1)} collective-permute-done((f32[32,2048]{1,0:T(8,128)S(1)}, f32[32,2048]{1,0:T(8,128)S(1)}, u32[]{:S(2)}, u32[]{:S(2)}) %collective-permute-start.11) | collective-permute-done | bytes 262176 | tf_op jit(solution)/shard_map/ppermute | solution.py:19
  190.1 11.8 %collective-permute-done.12 = f32[32,2048]{1,0:T(8,128)S(1)} collective-permute-done((f32[32,2048]{1,0:T(8,128)S(1)}, f32[32,2048]{1,0:T(8,128)S(1)}, u32[]{:S(2)}, u32[]{:S(2)}) %collective-permute-start.12) | collective-permute-done | bytes 262176 | tf_op jit(solution)/shard_map/ppermute | solution.py:19
  206.8 14.4 %collective-permute-done.13 = f32[32,2048]{1,0:T(8,128)S(1)} collective-permute-done((f32[32,2048]{1,0:T(8,128)S(1)}, f32[32,2048]{1,0:T(8,128)S(1)}, u32[]{:S(2)}, u32[]{:S(2)}) %collective-permute-start.13) | collective-permute-done | bytes 262176 | tf_op jit(solution)/shard_map/ppermute | solution.py:19
  224.4 6.1 collective-permute-done.14
  238.8 13.1 %collective-permute-done.16 = f32[32,4096]{1,0:T(8,128)S(1)} collective-permute-done((f32[32,4096]{1,0:T(8,128)S(1)}, f32[32,4096]{1,0:T(8,128)S(1)}, u32[]{:S(2)}, u32[]{:S(2)}) %collective-permute-start.16) | collective-permute-done | bytes 524320 | tf_op jit(solution)/shard_map/ppermute | solution.py:19
  256.1 23.0 %collective-permute-done.17 = f32[32,4096]{1,0:T(8,128)S(1)} collective-permute-done((f32[32,4096]{1,0:T(8,128)S(1)}, f32[32,4096]{1,0:T(8,128)S(1)}, u32[]{:S(2)}, u32[]{:S(2)}) %collective-permute-start.17) | collective-permute-done | bytes 524320 | tf_op jit(solution)/shard_map/ppermute | solution.py:19
  283.8 25.9 %collective-permute-done.18 = f32[32,4096]{1,0:T(8,128)S(1)} collective-permute-done((f32[32,4096]{1,0:T(8,128)S(1)}, f32[32,4096]{1,0:T(8,128)S(1)}, u32[]{:S(2)}, u32[]{:S(2)}) %collective-permute-start.18) | collective-permute-done | bytes 524320 | tf_op jit(solution)/shard_map/ppermute | solution.py:19
  312.8 11.8 %collective-permute-done.19 = f32[32,4096]{1,0:T(8,128)S(1)} collective-permute-done((f32[32,4096]{1,0:T(8,128)S(1)}, f32[32,4096]{1,0:T(8,128)S(1)}, u32[]{:S(2)}, u32[]{:S(2)}) %collective-permute-start.19) | collective-permute-done | bytes 524320 | tf_op jit(solution)/shard_map/ppermute | solution.py:19
  329.3 10.8 %collective-permute-done.20 = f32[32,4096]{1,0:T(8,128)S(1)} collective-permute-done((f32[32,4096]{1,0:T(8,128)S(1)}, f32[32,4096]{1,0:T(8,128)S(1)}, u32[]{:S(2)}, u32[]{:S(2)}) %collective-permute-start.20) | collective-permute-done | bytes 524320 | tf_op jit(solution)/shard_map/ppermute | solution.py:19
  350.4 13.1 %collective-permute-done.22 = f32[32,4096]{1,0:T(8,128)S(1)} collective-permute-done((f32[32,4096]{1,0:T(8,128)S(1)}, f32[32,4096]{1,0:T(8,128)S(1)}, u32[]{:S(2)}, u32[]{:S(2)}) %collective-permute-start.22) | collective-permute-done | bytes 524320 | tf_op jit(solution)/shard_map/ppermute | solution.py:19
  368.6 22.7 %collective-permute-done.23 = f32[32,4096]{1,0:T(8,128)S(1)} collective-permute-done((f32[32,4096]{1,0:T(8,128)S(1)}, f32[32,4096]{1,0:T(8,128)S(1)}, u32[]{:S(2)}, u32[]{:S(2)}) %collective-permute-start.23) | collective-permute-done | bytes 524320 | tf_op jit(solution)/shard_map/ppermute | solution.py:19
  395.7 25.9 %collective-permute-done.24 = f32[32,4096]{1,0:T(8,128)S(1)} collective-permute-done((f32[32,4096]{1,0:T(8,128)S(1)}, f32[32,4096]{1,0:T(8,128)S(1)}, u32[]{:S(2)}, u32[]{:S(2)}) %collective-permute-start.24) | collective-permute-done | bytes 524320 | tf_op jit(solution)/shard_map/ppermute | solution.py:19
  424.8 11.7 %collective-permute-done.25 = f32[32,4096]{1,0:T(8,128)S(1)} collective-permute-done((f32[32,4096]{1,0:T(8,128)S(1)}, f32[32,4096]{1,0:T(8,128)S(1)}, u32[]{:S(2)}, u32[]{:S(2)}) %collective-permute-start.25) | collective-permute-done | bytes 524320 | tf_op jit(solution)/shard_map/ppermute | solution.py:19
  441.5 10.5 %collective-permute-done.26 = f32[32,4096]{1,0:T(8,128)S(1)} collective-permute-done((f32[32,4096]{1,0:T(8,128)S(1)}, f32[32,4096]{1,0:T(8,128)S(1)}, u32[]{:S(2)}, u32[]{:S(2)}) %collective-permute-start.26) | collective-permute-done | bytes 524320 | tf_op jit(solution)/shard_map/ppermute | solution.py:19
  460.9 7.5 %collective-permute-done.28 = f32[32,2048]{1,0:T(8,128)S(1)} collective-permute-done((f32[32,2048]{1,0:T(8,128)S(1)}, f32[32,2048]{1,0:T(8,128)S(1)}, u32[]{:S(2)}, u32[]{:S(2)}) %collective-permute-start.28) | collective-permute-done | bytes 262176 | tf_op jit(solution)/shard_map/ppermute | solution.py:19
  473.5 11.5 %collective-permute-done.29 = f32[32,2048]{1,0:T(8,128)S(1)} collective-permute-done((f32[32,2048]{1,0:T(8,128)S(1)}, f32[32,2048]{1,0:T(8,128)S(1)}, u32[]{:S(2)}, u32[]{:S(2)}) %collective-permute-start.29) | collective-permute-done | bytes 262176 | tf_op jit(solution)/shard_map/ppermute | solution.py:19
  490.0 14.6 %collective-permute-done.30 = f32[32,2048]{1,0:T(8,128)S(1)} collective-permute-done((f32[32,2048]{1,0:T(8,128)S(1)}, f32[32,2048]{1,0:T(8,128)S(1)}, u32[]{:S(2)}, u32[]{:S(2)}) %collective-permute-start.30) | collective-permute-done | bytes 262176 | tf_op jit(solution)/shard_map/ppermute | solution.py:19
  541.6 8.0 %collective-permute-done.35 = f32[32,1024]{1,0:T(8,128)S(1)} collective-permute-done((f32[32,1024]{1,0:T(8,128)S(1)}, f32[32,1024]{1,0:T(8,128)S(1)}, u32[]{:S(2)}, u32[]{:S(2)}) %collective-permute-start.35) | collective-permute-done | bytes 131104 | tf_op jit(solution)/shard_map/ppermute | solution.py:19
  561.2 6.9 %all-to-all-start.1 = ((f32[8,1,1792]{2,1,0:T(1,128)}), f32[8,1,1792]{2,1,0:T(1,128)}, u32[]{:S(2)}, u32[]{:S(2)}) async-start(f32[8,1,1792]{2,1,0:T(1,128)} %reshape.100), calls=%async_computation.1 | async-start | bytes 114688 | tf_op jit(solution)/shard_map/all_to_all | solution.py:92
  569.1 6.3 %collective-permute-start.38 = (f32[32,512]{1,0:T(8,128)S(1)}, f32[32,512]{1,0:T(8,128)S(1)}, u32[]{:S(2)}, u32[]{:S(2)}) collective-permute-start(f32[32,512]{1,0:T(8,128)S(1)} %add.522), channel_id=1, source_target_pairs={{0,32},{32,0},{8,40},{40,8},{16,48},{48,16},{24,56},{56,24},{64,96... | collective-permute-start | bytes 196616 | tf_op jit(solution)/shard_map/ppermute | solution.py:19
  599.2 6.6 %all-to-all-start.2 = ((f32[8,1,1792]{2,1,0:T(1,128)}), f32[8,1,1792]{2,1,0:T(1,128)S(1)}, u32[]{:S(2)}, u32[]{:S(2)}) async-start(f32[8,1,1792]{2,1,0:T(1,128)} %reshape.102), calls=%async_computation.2 | async-start | bytes 114688 | tf_op jit(solution)/shard_map/all_to_all | solution.py:93
  (292 shorter events, 292.8 us)
Async XLA Ops:
  2.9 38.4 %all-to-all-start = ((f32[8,1,1792]{2,1,0:T(1,128)}), f32[8,1,1792]{2,1,0:T(1,128)S(1)}, u32[]{:S(2)}, u32[]{:S(2)}) async-start(f32[8,1,1792]{2,1,0:T(1,128)} %reshape.98), calls=%async_computation | async-start | bytes 114688 | tf_op jit(solution)/shard_map/all_to_all | solution.py:37
  58.3 31.3 %collective-permute-start = (f32[32,128]{1,0:T(8,128)}, f32[32,128]{1,0:T(8,128)}, u32[]{:S(2)}, u32[]{:S(2)}) collective-permute-start(f32[32,128]{1,0:T(8,128)} %slice_subtract_fusion), channel_id=1, source_target_pairs={{0,8},{8,0},{16,24},{24,16},{32,40},{40,32},{48,56},{56,48},{64,72... | collective-permute-start | bytes 49160 | tf_op jit(solution)/shard_map/ppermute | solution.py:19
  142.9 10.4 %collective-permute-start.8 = (f32[32,1024]{1,0:T(8,128)S(1)}, f32[32,1024]{1,0:T(8,128)S(1)}, u32[]{:S(2)}, u32[]{:S(2)}) collective-permute-start(f32[32,1024]{1,0:T(8,128)S(1)} %add.463), channel_id=1, source_target_pairs={{0,32},{32,0},{8,40},{40,8},{16,48},{48,16},{24,56},{56,24},{64,96... | collective-permute-start | bytes 393224 | tf_op jit(solution)/shard_map/ppermute | solution.py:19
  153.3 10.7 %collective-permute-start.9 = (f32[32,1024]{1,0:T(8,128)S(1)}, f32[32,1024]{1,0:T(8,128)S(1)}, u32[]{:S(2)}, u32[]{:S(2)}) collective-permute-start(f32[32,1024]{1,0:T(8,128)S(1)} %add.464), channel_id=1, source_target_pairs={{0,64},{64,0},{8,72},{72,8},{16,80},{80,16},{24,88},{88,24},{32,96... | collective-permute-start | bytes 393224 | tf_op jit(solution)/shard_map/ppermute | solution.py:19
  185.9 16.0 %collective-permute-start.12 = (f32[32,2048]{1,0:T(8,128)S(1)}, f32[32,2048]{1,0:T(8,128)S(1)}, u32[]{:S(2)}, u32[]{:S(2)}) collective-permute-start(f32[32,2048]{1,0:T(8,128)S(1)} %add.479), channel_id=1, source_target_pairs={{0,32},{32,0},{8,40},{40,8},{16,48},{48,16},{24,56},{56,24},{64,96... | collective-permute-start | bytes 786440 | tf_op jit(solution)/shard_map/ppermute | solution.py:19
  201.9 19.4 %collective-permute-start.13 = (f32[32,2048]{1,0:T(8,128)S(1)}, f32[32,2048]{1,0:T(8,128)S(1)}, u32[]{:S(2)}, u32[]{:S(2)}) collective-permute-start(f32[32,2048]{1,0:T(8,128)S(1)} %add.480), channel_id=1, source_target_pairs={{0,64},{64,0},{8,72},{72,8},{16,80},{80,16},{24,88},{88,24},{32,96... | collective-permute-start | bytes 786440 | tf_op jit(solution)/shard_map/ppermute | solution.py:19
  236.9 15.0 %collective-permute-start.16 = (f32[32,4096]{1,0:T(8,128)S(1)}, f32[32,4096]{1,0:T(8,128)S(1)}, u32[]{:S(2)}, u32[]{:S(2)}) collective-permute-start(f32[32,4096]{1,0:T(8,128)S(1)} %add.497), channel_id=1, source_target_pairs={{0,16},{16,0},{8,24},{24,8},{32,48},{48,32},{40,56},{56,40},{64,80... | collective-permute-start | bytes 1572872 | tf_op jit(solution)/shard_map/ppermute | solution.py:19
  251.9 27.1 %collective-permute-start.17 = (f32[32,4096]{1,0:T(8,128)S(1)}, f32[32,4096]{1,0:T(8,128)S(1)}, u32[]{:S(2)}, u32[]{:S(2)}) collective-permute-start(f32[32,4096]{1,0:T(8,128)S(1)} %add.498), channel_id=1, source_target_pairs={{0,32},{32,0},{8,40},{40,8},{16,48},{48,16},{24,56},{56,24},{64,96... | collective-permute-start | bytes 1572872 | tf_op jit(solution)/shard_map/ppermute | solution.py:19
  279.1 30.6 %collective-permute-start.18 = (f32[32,4096]{1,0:T(8,128)S(1)}, f32[32,4096]{1,0:T(8,128)S(1)}, u32[]{:S(2)}, u32[]{:S(2)}) collective-permute-start(f32[32,4096]{1,0:T(8,128)S(1)} %add.499), channel_id=1, source_target_pairs={{0,64},{64,0},{8,72},{72,8},{16,80},{80,16},{24,88},{88,24},{32,96... | collective-permute-start | bytes 1572872 | tf_op jit(solution)/shard_map/ppermute | solution.py:19
  309.7 14.9 %collective-permute-start.19 = (f32[32,4096]{1,0:T(8,128)S(1)}, f32[32,4096]{1,0:T(8,128)S(1)}, u32[]{:S(2)}, u32[]{:S(2)}) collective-permute-start(f32[32,4096]{1,0:T(8,128)S(1)} %add.500), channel_id=1, source_target_pairs={{0,128},{128,0},{8,136},{136,8},{16,144},{144,16},{24,152},{152,24... | collective-permute-start | bytes 1572872 | tf_op jit(solution)/shard_map/ppermute | solution.py:19
  324.7 15.5 %collective-permute-start.20 = (f32[32,4096]{1,0:T(8,128)S(1)}, f32[32,4096]{1,0:T(8,128)S(1)}, u32[]{:S(2)}, u32[]{:S(2)}) collective-permute-start(f32[32,4096]{1,0:T(8,128)S(1)} %add.501), channel_id=1, source_target_pairs={{0,256},{256,0},{8,264},{264,8},{16,272},{272,16},{24,280},{280,24... | collective-permute-start | bytes 1572872 | tf_op jit(solution)/shard_map/ppermute | solution.py:19
  348.4 15.0 %collective-permute-start.22 = (f32[32,4096]{1,0:T(8,128)S(1)}, f32[32,4096]{1,0:T(8,128)S(1)}, u32[]{:S(2)}, u32[]{:S(2)}) collective-permute-start(f32[32,4096]{1,0:T(8,128)S(1)} %add.503), channel_id=1, source_target_pairs={{0,16},{16,0},{8,24},{24,8},{32,48},{48,32},{40,56},{56,40},{64,80... | collective-permute-start | bytes 1572872 | tf_op jit(solution)/shard_map/ppermute | solution.py:19
  363.5 27.9 %collective-permute-start.23 = (f32[32,4096]{1,0:T(8,128)S(1)}, f32[32,4096]{1,0:T(8,128)S(1)}, u32[]{:S(2)}, u32[]{:S(2)}) collective-permute-start(f32[32,4096]{1,0:T(8,128)S(1)} %add.504), channel_id=1, source_target_pairs={{0,32},{32,0},{8,40},{40,8},{16,48},{48,16},{24,56},{56,24},{64,96... | collective-permute-start | bytes 1572872 | tf_op jit(solution)/shard_map/ppermute | solution.py:19
  391.4 30.1 %collective-permute-start.24 = (f32[32,4096]{1,0:T(8,128)S(1)}, f32[32,4096]{1,0:T(8,128)S(1)}, u32[]{:S(2)}, u32[]{:S(2)}) collective-permute-start(f32[32,4096]{1,0:T(8,128)S(1)} %add.505), channel_id=1, source_target_pairs={{0,64},{64,0},{8,72},{72,8},{16,80},{80,16},{24,88},{88,24},{32,96... | collective-permute-start | bytes 1572872 | tf_op jit(solution)/shard_map/ppermute | solution.py:19
  421.6 14.9 %collective-permute-start.25 = (f32[32,4096]{1,0:T(8,128)S(1)}, f32[32,4096]{1,0:T(8,128)S(1)}, u32[]{:S(2)}, u32[]{:S(2)}) collective-permute-start(f32[32,4096]{1,0:T(8,128)S(1)} %add.506), channel_id=1, source_target_pairs={{0,128},{128,0},{8,136},{136,8},{16,144},{144,16},{24,152},{152,24... | collective-permute-start | bytes 1572872 | tf_op jit(solution)/shard_map/ppermute | solution.py:19
  436.6 15.5 %collective-permute-start.26 = (f32[32,4096]{1,0:T(8,128)S(1)}, f32[32,4096]{1,0:T(8,128)S(1)}, u32[]{:S(2)}, u32[]{:S(2)}) collective-permute-start(f32[32,4096]{1,0:T(8,128)S(1)} %add.507), channel_id=1, source_target_pairs={{0,256},{256,0},{8,264},{264,8},{16,272},{272,16},{24,280},{280,24... | collective-permute-start | bytes 1572872 | tf_op jit(solution)/shard_map/ppermute | solution.py:19
  468.4 16.6 %collective-permute-start.29 = (f32[32,2048]{1,0:T(8,128)S(1)}, f32[32,2048]{1,0:T(8,128)S(1)}, u32[]{:S(2)}, u32[]{:S(2)}) collective-permute-start(f32[32,2048]{1,0:T(8,128)S(1)} %add.510), channel_id=1, source_target_pairs={{0,32},{32,0},{8,40},{40,8},{16,48},{48,16},{24,56},{56,24},{64,96... | collective-permute-start | bytes 786440 | tf_op jit(solution)/shard_map/ppermute | solution.py:19
  485.1 19.6 %collective-permute-start.30 = (f32[32,2048]{1,0:T(8,128)S(1)}, f32[32,2048]{1,0:T(8,128)S(1)}, u32[]{:S(2)}, u32[]{:S(2)}) collective-permute-start(f32[32,2048]{1,0:T(8,128)S(1)} %add.511), channel_id=1, source_target_pairs={{0,64},{64,0},{8,72},{72,8},{16,80},{80,16},{24,88},{88,24},{32,96... | collective-permute-start | bytes 786440 | tf_op jit(solution)/shard_map/ppermute | solution.py:19
  526.2 11.0 %collective-permute-start.34 = (f32[32,1024]{1,0:T(8,128)S(1)}, f32[32,1024]{1,0:T(8,128)S(1)}, u32[]{:S(2)}, u32[]{:S(2)}) collective-permute-start(f32[32,1024]{1,0:T(8,128)S(1)} %add.516), channel_id=1, source_target_pairs={{0,32},{32,0},{8,40},{40,8},{16,48},{48,16},{24,56},{56,24},{64,96... | collective-permute-start | bytes 393224 | tf_op jit(solution)/shard_map/ppermute | solution.py:19
  537.2 12.4 %collective-permute-start.35 = (f32[32,1024]{1,0:T(8,128)S(1)}, f32[32,1024]{1,0:T(8,128)S(1)}, u32[]{:S(2)}, u32[]{:S(2)}) collective-permute-start(f32[32,1024]{1,0:T(8,128)S(1)} %add.517), channel_id=1, source_target_pairs={{0,64},{64,0},{8,72},{72,8},{16,80},{80,16},{24,88},{88,24},{32,96... | collective-permute-start | bytes 393224 | tf_op jit(solution)/shard_map/ppermute | solution.py:19
  555.8 12.4 %collective-permute-start.37 = (f32[32,512]{1,0:T(8,128)}, f32[32,512]{1,0:T(8,128)}, u32[]{:S(2)}, u32[]{:S(2)}) collective-permute-start(f32[32,512]{1,0:T(8,128)} %add.521), channel_id=1, source_target_pairs={{0,16},{16,0},{8,24},{24,8},{32,48},{48,32},{40,56},{56,40},{64,80... | collective-permute-start | bytes 196616 | tf_op jit(solution)/shard_map/ppermute | solution.py:19
  561.2 38.0 %all-to-all-start.1 = ((f32[8,1,1792]{2,1,0:T(1,128)}), f32[8,1,1792]{2,1,0:T(1,128)}, u32[]{:S(2)}, u32[]{:S(2)}) async-start(f32[8,1,1792]{2,1,0:T(1,128)} %reshape.100), calls=%async_computation.1 | async-start | bytes 114688 | tf_op jit(solution)/shard_map/all_to_all | solution.py:92
  569.1 9.9 %collective-permute-start.38 = (f32[32,512]{1,0:T(8,128)S(1)}, f32[32,512]{1,0:T(8,128)S(1)}, u32[]{:S(2)}, u32[]{:S(2)}) collective-permute-start(f32[32,512]{1,0:T(8,128)S(1)} %add.522), channel_id=1, source_target_pairs={{0,32},{32,0},{8,40},{40,8},{16,48},{48,16},{24,56},{56,24},{64,96... | collective-permute-start | bytes 196616 | tf_op jit(solution)/shard_map/ppermute | solution.py:19
  599.2 13.8 %all-to-all-start.2 = ((f32[8,1,1792]{2,1,0:T(1,128)}), f32[8,1,1792]{2,1,0:T(1,128)S(1)}, u32[]{:S(2)}, u32[]{:S(2)}) async-start(f32[8,1,1792]{2,1,0:T(1,128)} %reshape.102), calls=%async_computation.2 | async-start | bytes 114688 | tf_op jit(solution)/shard_map/all_to_all | solution.py:93
  (42 other events, 684.6 us)
where the time goes:
time: 620 us; the launch traced here: 615 us
  waiting for transfers between devices  297 us (48%)
  starting transfers between devices  180 us (29%)
  other arithmetic  44.7 us (7%)
  local copies, waits for them, and re-layouts  41.1 us (7%)
  between operations  27.4 us (4%)
  matrix products  24 us (4%)
    ppermute x42, waiting for transfers between devices, from_partner(): return lax.ppermute(block, axis, route)  293 us
    ppermute x42, starting transfers between devices, from_partner(): return lax.ppermute(block, axis, route)  156 us
    dynamic_update_slice x40, other arithmetic, local(): lax.dynamic_update_slice(partial_value, current - piece, (0, column))  34.9 us
    dot_general x28, matrix products, contract_last(): lax.dot_general(left, right, (((1,), (1,)), ((), ())), precision=highest,...  15.3 us
  transfers between devices with their start and end apart: 45, of which 38 were waited for; matrix products, arithmetic and copies ran while one was open for 10% of the time, Pallas kernels for 0%

commit v1 on v0

v1 whole, which is shorter than its diff:
```python
import jax
import jax.numpy as jnp
from jax import lax
from jax.experimental import pallas as pl
from jax.experimental.pallas import tpu as pltpu
from jax.sharding import PartitionSpec as P

MESH = pl.DeviceIdType.MESH
LANES = 128
ONE_STEP = 3
NN = (((1,), (0,)), ((), ()))
NT = (((1,), (1,)), ((), ()))


def pair_slot(source, ancestor):
    return ancestor * (ancestor - 1) // 2 + source


def split(value):
    high = value.astype(jnp.bfloat16)
    low = (value - high.astype(jnp.float32)).astype(jnp.bfloat16)
    return high, low


def product(value, high, low, dims):
    rows = value.shape[0]
    value_high, value_low = split(value)
    both = lax.dot_general(
        jnp.concatenate([value_high, value_low], axis=0), high, dims, preferred_element_type=jnp.float32
    )
    rest = lax.dot_general(value_high, low, dims, preferred_element_type=jnp.float32)
    return both[:rows] + both[rows:] + rest


def scratch_plan(levels, pairs, rows, cols, group, slots):
    f32, bf16 = jnp.float32, jnp.bfloat16
    tile = (group, LANES)
    plan = {
        "diag32": pltpu.VMEM((2, rows, cols), f32),
        "off32": pltpu.VMEM((pairs, 2 * rows, 2 * LANES), f32),
        "diag_high": pltpu.VMEM((2 * rows, rows * 2**levels), bf16),
        "diag_low": pltpu.VMEM((2 * rows, rows * 2**levels), bf16),
        "off_high": pltpu.VMEM((pairs, 2 * rows, 2 * LANES), bf16),
        "off_low": pltpu.VMEM((pairs, 2 * rows, 2 * LANES), bf16),
        "tiles_v": pltpu.VMEM((2, 8, LANES), jnp.int32),
        "tiles_s": pltpu.SMEM((2, 8, LANES), jnp.int32),
    }
    for name in ("side", "fwd", "sol"):
        plan[name + "_out"] = pltpu.VMEM((slots,) + tile, f32)
        plan[name + "_in"] = pltpu.VMEM((slots,) + tile, f32)
    for name in ("b", "y", "w", "x"):
        plan[name] = pltpu.VMEM((levels,) + tile, f32)
    moves = ["side", "fwd", "sol", "diag0", "diag1", "off0", "off1", "tiles"]
    for level in range(1, levels):
        count = 2 ** (level - 1)
        plan[f"acc{level}"] = pltpu.VMEM((count,) + tile, f32)
        plan[f"full{level}"] = pltpu.VMEM((count,) + tile, f32)
        if level < 2:
            continue
        plan[f"part{level}"] = pltpu.VMEM((count,) + tile, f32)
        if level <= ONE_STEP:
            plan[f"up{level}"] = pltpu.VMEM((count, count) + tile, f32)
            plan[f"down{level}"] = pltpu.VMEM((count, count) + tile, f32)
            moves += [f"up{level}", f"down{level}"]
        else:
            plan[f"up{level}"] = pltpu.VMEM((count,) + tile, f32)
            plan[f"down{level}"] = pltpu.VMEM((count,) + tile, f32)
            plan[f"sum{level}"] = pltpu.VMEM((count,) + tile, f32)
            moves += [f"up{level}", f"down{level}", f"sum{level}", f"full{level}"]
    plan["send_sem"] = pltpu.SemaphoreType.DMA((len(moves),))
    plan["recv_sem"] = pltpu.SemaphoreType.DMA((len(moves),))
    plan["local_sem"] = pltpu.SemaphoreType.DMA((5,))
    return plan, moves


def make_kernel(levels, names, moves, rows, cols, group, grid):
    chunk = rows // grid
    slots = 2 * grid
    top = levels - 1
    chips = 2 ** (top - 1)
    low_cols = 1024
    low_pairs = 6

    def kernel(side_ref, diag_hbm, off_hbm, tile_ref, fwd_ref, sol_ref, *scratch):
        at = dict(zip(names, scratch))
        send_sem, recv_sem, local_sem = at["send_sem"], at["recv_sem"], at["local_sem"]
        slot_of = {name: place for place, name in enumerate(moves)}
        leaf, z = lax.axis_index("leaf"), lax.axis_index("grid")
        core = lax.rem(leaf, 2)
        chip = leaf // 2
        lane = lax.broadcasted_iota(jnp.int32, (group, LANES), 1)
        lane_block = lane // chunk
        left_half = lane < rows
        own_rhs = 2 * z + core
        own_rows = core * grid + z

        def column_peer(step):
            index = lax.rem(own_rhs + step, slots)
            return index, (2 * chip + lax.rem(index, 2), index // 2)

        def row_peer(step):
            index = lax.rem(own_rows + step, slots)
            return index, (2 * chip + index // grid, lax.rem(index, grid))

        def plane_peer(count, step):
            place = lax.rem(chip, count)
            index = lax.rem(place + step, count)
            return index, (2 * (chip - place + index) + core, z)

        def send(name, source, target, device):
            pltpu.make_async_remote_copy(
                src_ref=source,
                dst_ref=target,
                send_sem=send_sem.at[slot_of[name]],
                recv_sem=recv_sem.at[slot_of[name]],
                device_id=device,
                device_id_type=MESH,
            ).start()

        def await_bytes(view, sem):
            pltpu.make_async_copy(view, view, sem).wait()

        sent = []

        def received(name, view):
            await_bytes(view, recv_sem.at[slot_of[name]])
            sent.append((name, view))

        diag32, off32 = at["diag32"], at["off32"]
        low = pl.ds(0, low_cols)
        high = pl.ds(low_cols, cols - low_cols)
        mine = pl.ds(pl.multiple_of(core * rows, rows), rows)
        pairs = off_hbm.shape[0]
        low_p, high_p = pl.ds(0, low_pairs), pl.ds(low_pairs, pairs - low_pairs)
        parts = [
            ("diag0", diag_hbm.at[:, low], diag32.at[core, :, low]),
            ("off0", off_hbm.at[low_p], off32.at[low_p, mine, :]),
            ("off1", off_hbm.at[high_p], off32.at[high_p, mine, :]),
            ("diag1", diag_hbm.at[:, high], diag32.at[core, :, high]),
        ]
        own_copies = {}
        for place, (name, source, target) in enumerate(parts):
            own_copies[name] = pltpu.make_async_copy(source, target, local_sem.at[place])
            own_copies[name].start()

        barrier = pltpu.get_barrier_semaphore()

        def greet_column(step, carry):
            _, device = column_peer(step)
            pl.semaphore_signal(barrier, inc=1, device_id=device, device_id_type=MESH)
            return carry

        def greet_plane(step, carry):
            _, device = plane_peer(chips, step)
            pl.semaphore_signal(barrier, inc=1, device_id=device, device_id_type=MESH)
            return carry

        lax.fori_loop(1, slots, greet_column, 0)
        lax.fori_loop(1, chips, greet_plane, 0)

        used = levels * chunk
        side = side_ref[...].reshape(used, slots * group)
        side = jnp.concatenate([side, jnp.zeros((LANES - used, slots * group), jnp.float32)], axis=0)
        at["side_out"][...] = side.T.reshape(slots, group, LANES)
        at["tiles_v"][core] = tile_ref[...]
        for level in range(1, levels):
            at[f"acc{level}"][...] = jnp.zeros_like(at[f"acc{level}"])
        at["w"][...] = jnp.zeros_like(at["w"])

        pl.semaphore_wait(barrier, slots - 1 + chips - 1)

        def send_side(step, carry):
            index, device = column_peer(step)
            send("side", at["side_out"].at[index], at["side_in"].at[own_rows], device)
            return carry

        partner = (2 * chip + 1 - core, z)
        send("tiles", tile_ref, at["tiles_v"].at[core], partner)
        name, source, target = parts[0]
        send(name, source, target, partner)
        lax.fori_loop(1, slots, send_side, 0)
        for name, source, target in parts[1:]:
            send(name, source, target, partner)
        at["side_in"][own_rows] = at["side_out"][own_rhs]

        other = pl.ds(pl.multiple_of((1 - core) * rows, rows), rows)
        theirs = {
            "diag0": diag32.at[1 - core, :, low],
            "off0": off32.at[low_p, other, :],
            "off1": off32.at[high_p, other, :],
            "diag1": diag32.at[1 - core, :, high],
        }

        def arrived(name):
            own_copies[name].wait()
            received(name, theirs[name])

        def put_diag(half, place, value):
            value_high, value_low = split(value)
            spot = pl.ds(half * rows, rows)
            at["diag_high"][spot, place] = value_high
            at["diag_low"][spot, place] = value_low

        wide_lane = lax.broadcasted_iota(jnp.int32, (rows, LANES), 1)

        def convert_diag(first, last):
            def block(j, carry):
                here = pl.ds(pl.multiple_of(j * LANES, LANES), LANES)
                before = pl.ds(pl.multiple_of((j - 1) * LANES, LANES), LANES)
                for half in range(2):
                    mixed = jnp.where(wide_lane < rows, diag32[half, :, here], diag32[half, :, before])
                    put_diag(half, here, pltpu.roll(mixed, rows, 1))
                return carry

            lax.fori_loop(first, last, block, 0)

        def convert_last_diag():
            j = cols // LANES
            for half in range(2):
                tail = diag32[half, :, j * LANES : cols]
                tail = jnp.concatenate([tail, jnp.zeros((rows, LANES - rows), jnp.float32)], axis=1)
                mixed = jnp.where(wide_lane < rows, tail, diag32[half, :, (j - 1) * LANES : j * LANES])
                put_diag(half, pl.ds(j * LANES, LANES), pltpu.roll(mixed, rows, 1))

        def convert_off(first, last):
            def block(p, carry):
                value_high, value_low = split(off32[p])
                at["off_high"][p] = value_high
                at["off_low"][p] = value_low
                return carry

            lax.fori_loop(first, last, block, 0)

        arrived("diag0")
        for half in range(2):
            first = jnp.where(wide_lane < rows, diag32[half, :, 0:LANES], 0.0)
            put_diag(half, pl.ds(0, LANES), first if half == 0 else pltpu.roll(first, rows, 1))
        convert_diag(1, low_cols // LANES)
        arrived("off0")
        convert_off(0, low_pairs)
        received("tiles", at["tiles_v"].at[1 - core])
        to_smem = pltpu.make_async_copy(at["tiles_v"], at["tiles_s"], local_sem.at[4])
        to_smem.start()
        to_smem.wait()
        tiles = at["tiles_s"]

        received("side", at["side_in"].at[pl.ds(0, slots - 1)])
        turned = []
        for s in range(slots):
            value = at["side_in"][s]
            turned.append(pltpu.roll(value, s * chunk, 1) if s else value)
        for level in range(levels):
            value = turned[0]
            for s in range(1, slots):
                value = jnp.where(lane_block == (s + level) % slots, turned[s], value)
            at["b"][level] = pltpu.roll(value, LANES - level * chunk, 1) if level else value

        def diag_block(level):
            if level == 0:
                place = pl.ds(0, LANES)
            else:
                place = pl.ds(rows * 2**level, rows * 2**level)
            return at["diag_high"][:, place], at["diag_low"][:, place]

        def contribute(source, level):
            p = pair_slot(source, level)
            known = at["y"][source]
            stacked = jnp.concatenate([jnp.where(left_half, known, 0.0), jnp.where(left_half, 0.0, known)], axis=0)
            out = product(stacked, at["off_high"][p], at["off_low"][p], NN)
            pieces = []
            for half in range(2):
                for t in range(2):
                    piece = out[half * group : (half + 1) * group, t * LANES : (t + 1) * LANES]
                    pieces.append((piece, tiles[half, t, p]))
            acc = at[f"acc{level}"]
            count = 2 ** (level - 1)

            def add(target, carry):
                value = acc[target]
                for piece, number in pieces:
                    value = value - piece * (number == target).astype(jnp.float32)
                acc[target] = value
                return carry

            if count <= 4:
                for target in range(count):
                    add(target, 0)
            else:
                lax.fori_loop(0, count, add, 0)

        def gather_known(ancestor, level):
            p = pair_slot(level, ancestor)
            full = at[f"full{ancestor}"]
            halves = []
            for half in range(2):
                halves.append(jnp.concatenate([full[tiles[half, t, p]] for t in range(2)], axis=1))
            out = product(jnp.concatenate(halves, axis=0), at["off_high"][p], at["off_low"][p], NT)
            at["w"][level] += jnp.where(left_half, out[:group], out[group:])

        def broadcast(name, source, level):
            count = 2 ** (level - 1)
            place = lax.rem(chip, count)
            target = at[name]

            def one(step, carry):
                _, device = plane_peer(count, step)
                send(name, source, target.at[place], device)
                return carry

            lax.fori_loop(1, count, one, 0)

        def scatter(name, source, level):
            count = 2 ** (level - 1)
            place = lax.rem(chip, count)
            target = at[name]

            def one(step, carry):
                index, device = plane_peer(count, step)
                send(name, source.at[index], target.at[place], device)
                return carry

            lax.fori_loop(1, count, one, 0)

        def await_all(name, level):
            count = 2 ** (level - 1)
            received(name, at[name].at[pl.ds(0, count - 1)])

        def total(ref, count):
            value = ref[0]
            for place in range(1, count):
                value = value + ref[place]
            return value

        at["y"][0] = product(at["b"][0], *diag_block(0), NT)
        contribute(0, 1)
        at["y"][1] = product(at["b"][1] + at["acc1"][0], *diag_block(1), NT)
        contribute(0, 2)
        for level in range(2, levels):
            count = 2 ** (level - 1)
            place = lax.rem(chip, count)
            contribute(level - 1, level)
            acc, up = at[f"acc{level}"], at[f"up{level}"]
            if level <= ONE_STEP:
                acc[place] += at["b"][level]
                broadcast(f"up{level}", acc, level)
                up[place] = acc[...]
            else:
                scatter(f"up{level}", acc, level)
                up[place] = acc[place]
            if level == 2:
                for source in range(level):
                    contribute(source, level + 1) if level < top else None
                arrived("off1")
                convert_off(low_pairs, pairs)
            else:
                if level < top:
                    for source in range(level):
                        contribute(source, level + 1)
                if level == 3:
                    arrived("diag1")
                    convert_diag(low_cols // LANES, 2 * low_cols // LANES)
            await_all(f"up{level}", level)
            if level <= ONE_STEP:
                whole = total(up, count)
            else:
                summed = at[f"sum{level}"]
                summed[place] = at["b"][level] + total(up, count)
                broadcast(f"sum{level}", summed.at[place], level)
                if level == top - 2:
                    convert_diag(rows * 2 ** (level + 1) // LANES, rows * 2 ** (level + 2) // LANES)
                if level == top - 1:
                    convert_diag(rows * 2 ** (level + 1) // LANES, rows * 2 ** (level + 2) // LANES - 1)
                    convert_last_diag()
                await_all(f"sum{level}", level)
                whole = summed[...]
            whole = jnp.concatenate([whole[t] for t in range(count)], axis=1)
            at["y"][level] = product(whole, *diag_block(level), NT)

        def pack(values, name):
            turned = []
            for level in range(levels):
                value = values[level]
                turned.append(pltpu.roll(value, level * chunk, 1) if level else value)
            for s in range(slots):
                value = turned[0]
                for level in range(1, levels):
                    value = jnp.where(lane_block == (s + level) % slots, turned[level], value)
                at[name + "_out"][s] = pltpu.roll(value, LANES - s * chunk, 1) if s else value

            def one(step, carry):
                index, device = row_peer(step)
                send(name, at[name + "_out"].at[index], at[name + "_in"].at[own_rhs], device)
                return carry

            lax.fori_loop(1, slots, one, 0)
            at[name + "_in"][own_rhs] = at[name + "_out"][own_rows]

        def unpack(name, target):
            received(name, at[name + "_in"].at[pl.ds(0, slots - 1)])
            value = at[name + "_in"][...].reshape(slots * group, LANES).T
            for level in range(levels):
                target[level] = value[level * chunk : (level + 1) * chunk]

        for level in reversed(range(levels)):
            residue = at["y"][level] - at["w"][level]
            value = product(residue, *diag_block(level), NN)
            if level < 2:
                at["x"][level] = value
                if level == 1:
                    at["full1"][0] = value
                    gather_known(1, 0)
                continue
            count = 2 ** (level - 1)
            place = lax.rem(chip, count)
            part, down, full = at[f"part{level}"], at[f"down{level}"], at[f"full{level}"]
            for t in range(count):
                part[t] = value[:, t * LANES : (t + 1) * LANES]
            later = [(level + 1, below) for below in reversed(range(level))] if level < top else []
            if level <= ONE_STEP:
                broadcast(f"down{level}", part, level)
                down[place] = part[...]
                for task in later:
                    gather_known(*task)
                await_all(f"down{level}", level)
                full[...] = total(down, count)
                at["x"][level] = full[place]
            else:
                scatter(f"down{level}", part, level)
                down[place] = part[place]
                if level == top:
                    pack(at["y"], "fwd")
                for task in later[:1]:
                    gather_known(*task)
                await_all(f"down{level}", level)
                value = total(down, count)
                at["x"][level] = value
                full[place] = value
                broadcast(f"full{level}", full.at[place], level)
                for task in later[1:]:
                    gather_known(*task)
                if level == top:
                    unpack("fwd", fwd_ref)
                await_all(f"full{level}", level)
            gather_known(level, level - 1)
            if level == 2:
                gather_known(2, 0)
        pack(at["x"], "sol")
        unpack("sol", sol_ref)
        for name, view in sent:
            await_bytes(view, send_sem.at[slot_of[name]])

    return kernel


def solution(mesh):
    grid = mesh.shape["grid"]

    def local(right_side, diag_inv, off_diag, tile_rows):
        levels, rhs, chunk = right_side.shape
        rows, cols = diag_inv.shape
        pairs = off_diag.shape[0]
        slots = 2 * grid
        group = rhs // slots
        side = jnp.transpose(right_side, (0, 2, 1))
        off = jnp.transpose(off_diag, (0, 2, 1))
        tiles = jnp.transpose(tile_rows[:, :, 0], (1, 0))
        tiles = jnp.pad(tiles, ((0, 8 - tiles.shape[0]), (0, LANES - pairs)))
        plan, moves = scratch_plan(levels, pairs, rows, cols, group, slots)
        vmem = pl.BlockSpec(memory_space=pltpu.VMEM)
        anywhere = pl.BlockSpec(memory_space=pl.ANY)
        out = jax.ShapeDtypeStruct(side.shape, jnp.float32)
        forward, backward = pl.pallas_call(
            make_kernel(levels, list(plan), moves, rows, cols, group, grid),
            out_shape=(out, out),
            in_specs=[vmem, anywhere, anywhere, vmem],
            out_specs=(vmem, vmem),
            scratch_shapes=list(plan.values()),
            compiler_params=pltpu.CompilerParams(
                collective_id=0, has_side_effects=True, vmem_limit_bytes=48 * 2**20
            ),
            name="tree_solve",
        )(side, diag_inv, off, tiles)
        return jnp.transpose(forward, (0, 2, 1)), jnp.transpose(backward, (0, 2, 1))

    in_specs = (
        P(None, None, ("leaf", "grid")),
        P("leaf", None),
        P(None, None, "leaf"),
        P(None, None, "leaf"),
    )
    out_specs = (P(None, None, ("leaf", "grid")), P(None, None, ("leaf", "grid")))
    return jax.shard_map(local, mesh=mesh, in_specs=in_specs, out_specs=out_specs, check_vma=False)
```

time: 620 us -> 139 us (0.22)
  waiting for transfers between devices: 297 us -> 0 us
  starting transfers between devices: 180 us -> 0 us
  Pallas kernels: 0 us -> 132 us
  other arithmetic: 44.7 us -> 0 us
  local copies, waits for them, and re-layouts: 41.1 us -> 5.68 us
  between operations: 27.4 us -> 0.64 us
  matrix products: 24 us -> 0 us
    ppermute x42 -> x0, waiting for transfers between devices: 293 us -> none  [from_partner(): return lax.ppermute(block, axis, route)]
    ppermute x42 -> x0, starting transfers between devices: 156 us -> none  [from_partner(): return lax.ppermute(block, axis, route)]
    pallas_call x0 -> x1, Pallas kernels: none -> 132 us  [local(): pl.pallas_call(make_kernel(levels, list(plan), moves, rows, cols, group,...]
    dynamic_update_slice x40 -> x0, other arithmetic: 34.9 us -> none  [local(): lax.dynamic_update_slice(partial_value, current - piece, (0, column))]
    all_to_all x3 -> x0, starting transfers between devices: 24.4 us -> none  [the longest x1 10.9 us: local(): lax.all_to_all(right_side, 'grid', split_axis=1, concat_axis=2, tiled=True)]
    dot_general x56 -> x0, matrix products: 24 us -> none  [the longest x28 15.3 us: contract_last(): lax.dot_general(left, right, (((1,), (1,)), ((), ())), precision=highest,...]
    squeeze x7 -> x0, local copies, waits for them, and re-layouts: 9.32 us -> none  [local(): local_side[height]]
    dynamic_update_slice x6 -> x0, local copies, waits for them, and re-layouts: 8.51 us -> none  [local(): lax.dynamic_update_slice(partial_value, local_side[height], (0, position))]
  transfers between devices with their start and end apart: 45 -> 0, of which waited for: 38 -> 0; matrix products, arithmetic and copies ran while one was open for 10% -> 0% of each run, Pallas kernels for 0% -> 0%
where the time goes in v1:
time: 139 us; the launch traced here: 138 us
  Pallas kernels  132 us (95%)
  local copies, waits for them, and re-layouts  5.68 us (4%)
    pallas_call x1, Pallas kernels, local(): pl.pallas_call(make_kernel(levels, list(plan), moves, rows, cols, group,...  132 us
    unnamed x8, local copies, waits for them, and re-layouts  4.99 us

profile of v1, /device:TPU:1, one launch (start us, length us, event | category | flops | bytes accessed | tf_op | source)
XLA Modules:
  0.0 138.5 jit_solution(7165027001013322736)
XLA Ops:
  0.6 0.7 pad.4.tile_ref
  1.3 0.0 copy-start
  1.3 1.6 %copy-done = f32[64,8128]{1,0:T(8,128)S(1)} copy-done((f32[64,8128]{1,0:T(8,128)S(1)}, f32[64,8128]{1,0:T(8,128)}, u32[]{:S(2)}) %copy-start) | copy-done | bytes 2080792
  2.9 0.0 copy-start.1
  2.9 1.3 copy-done.1
  4.2 0.0 copy-start.2
  4.2 0.8 copy-done.2
  5.1 132.2 %tree_solve.1 = (f32[7,8,256]{2,1,0:T(8,128)S(1)}, f32[7,8,256]{2,1,0:T(8,128)S(1)}) custom-call(f32[7,8,256]{2,1,0:T(8,128)S(1)} %bitcast.10, f32[64,8128]{1,0:T(8,128)S(1)} %copy-done, f32[21,64,256]{2,1,0:T(8,128)S(1)} %bitcast.7, s32[8,128]{1,0:T(8,128)S(1)} %pad.4.tile_ref), custom_call_target="tpu_custom_call" | custom-call | tf_op jit(solution)/shard_map/tree_solve/pallas_call | solution.py:472
  137.2 0.6 copy.8
  137.9 0.6 copy.9
Async XLA Ops:
  1.3 1.6 %copy-start = (f32[64,8128]{1,0:T(8,128)S(1)}, f32[64,8128]{1,0:T(8,128)}, u32[]{:S(2)}) copy-start(f32[64,8128]{1,0:T(8,128)} %diag_hbm.1) | copy-start | bytes 6242308
  2.9 1.3 copy-start.1
  4.2 0.8 copy-start.2

commit v2 on v1

--- a/solution.py
+++ b/solution.py
@@ -14,6 +14,11 @@
 
 def pair_slot(source, ancestor):
     return ancestor * (ancestor - 1) // 2 + source
+
+
+def outward(place, size):
+    away = (place + 1) // 2
+    return lax.rem(size // 2 + away * (1 - 2 * lax.rem(place, 2)) + size, size)
 
 
 def split(value):
@@ -42,9 +47,10 @@
         "diag_low": pltpu.VMEM((2 * rows, rows * 2**levels), bf16),
         "off_high": pltpu.VMEM((pairs, 2 * rows, 2 * LANES), bf16),
         "off_low": pltpu.VMEM((pairs, 2 * rows, 2 * LANES), bf16),
-        "tiles_v": pltpu.VMEM((2, 8, LANES), jnp.int32),
-        "tiles_s": pltpu.SMEM((2, 8, LANES), jnp.int32),
+        "tiles_v": pltpu.VMEM((2, 2, pairs), jnp.int32),
+        "tiles_s": pltpu.SMEM((2, 2, pairs), jnp.int32),
     }
+    plan["side32"] = pltpu.VMEM((levels, rows // (slots // 2), slots * group), f32)
     for name in ("side", "fwd", "sol"):
         plan[name + "_out"] = pltpu.VMEM((slots,) + tile, f32)
         plan[name + "_in"] = pltpu.VMEM((slots,) + tile, f32)
@@ -69,7 +75,7 @@
             moves += [f"up{level}", f"down{level}", f"sum{level}", f"full{level}"]
     plan["send_sem"] = pltpu.SemaphoreType.DMA((len(moves),))
     plan["recv_sem"] = pltpu.SemaphoreType.DMA((len(moves),))
-    plan["local_sem"] = pltpu.SemaphoreType.DMA((5,))
+    plan["local_sem"] = pltpu.SemaphoreType.DMA((7,))
     return plan, moves
 
 
@@ -80,8 +86,9 @@
     chips = 2 ** (top - 1)
     low_cols = 1024
     low_pairs = 6
-
-    def kernel(side_ref, diag_hbm, off_hbm, tile_ref, fwd_ref, sol_ref, *scratch):
+    ring = min(8, chips)
+
+    def kernel(side_hbm, diag_hbm, off_hbm, tile_hbm, fwd_ref, sol_ref, *scratch):
         at = dict(zip(names, scratch))
         send_sem, recv_sem, local_sem = at["send_sem"], at["recv_sem"], at["local_sem"]
         slot_of = {name: place for place, name in enumerate(moves)}
@@ -94,17 +101,27 @@
         own_rhs = 2 * z + core
         own_rows = core * grid + z
 
+        def column_device(step):
+            their_z = lax.rem(z + outward(step // 2, grid), grid)
+            their_core = lax.rem(core + 1 + lax.rem(step, 2), 2)
+            return their_core, their_z, (2 * chip + their_core, their_z)
+
         def column_peer(step):
-            index = lax.rem(own_rhs + step, slots)
-            return index, (2 * chip + lax.rem(index, 2), index // 2)
+            their_core, their_z, device = column_device(step)
+            return 2 * their_z + their_core, device
 
         def row_peer(step):
-            index = lax.rem(own_rows + step, slots)
-            return index, (2 * chip + index // grid, lax.rem(index, grid))
+            their_core, their_z, device = column_device(step)
+            return their_core * grid + their_z, device
 
         def plane_peer(count, step):
             place = lax.rem(chip, count)
-            index = lax.rem(place + step, count)
+            if count < ring:
+                index = lax.rem(place + outward(step, count), count)
+            else:
+                lines = count // ring
+                line = lax.rem(place // ring + outward(lax.rem(step, lines), lines), lines)
+                index = line * ring + lax.rem(place + outward(step // lines, ring), ring)
             return index, (2 * (chip - place + index) + core, z)
 
         def send(name, source, target, device):
@@ -132,6 +149,10 @@
         mine = pl.ds(pl.multiple_of(core * rows, rows), rows)
         pairs = off_hbm.shape[0]
         low_p, high_p = pl.ds(0, low_pairs), pl.ds(low_pairs, pairs - low_pairs)
+        load_side = pltpu.make_async_copy(side_hbm, at["side32"], local_sem.at[5])
+        load_side.start()
+        load_tiles = pltpu.make_async_copy(tile_hbm, at["tiles_v"].at[core], local_sem.at[6])
+        load_tiles.start()
         parts = [
             ("diag0", diag_hbm.at[:, low], diag32.at[core, :, low]),
             ("off0", off_hbm.at[low_p], off32.at[low_p, mine, :]),
@@ -155,14 +176,14 @@
             pl.semaphore_signal(barrier, inc=1, device_id=device, device_id_type=MESH)
             return carry
 
-        lax.fori_loop(1, slots, greet_column, 0)
-        lax.fori_loop(1, chips, greet_plane, 0)
+        lax.fori_loop(0, slots - 1, greet_column, 0)
+        lax.fori_loop(0, chips - 1, greet_plane, 0)
 
         used = levels * chunk
-        side = side_ref[...].reshape(used, slots * group)
+        load_side.wait()
+        side = at["side32"][...].reshape(used, slots * group)
         side = jnp.concatenate([side, jnp.zeros((LANES - used, slots * group), jnp.float32)], axis=0)
         at["side_out"][...] = side.T.reshape(slots, group, LANES)
-        at["tiles_v"][core] = tile_ref[...]
         for level in range(1, levels):
             at[f"acc{level}"][...] = jnp.zeros_like(at[f"acc{level}"])
         at["w"][...] = jnp.zeros_like(at["w"])
@@ -175,11 +196,9 @@
             return carry
 
         partner = (2 * chip + 1 - core, z)
-        send("tiles", tile_ref, at["tiles_v"].at[core], partner)
-        name, source, target = parts[0]
-        send(name, source, target, partner)
-        lax.fori_loop(1, slots, send_side, 0)
-        for name, source, target in parts[1:]:
+        send("tiles", tile_hbm, at["tiles_v"].at[core], partner)
+        lax.fori_loop(0, slots - 1, send_side, 0)
+        for name, source, target in parts:
             send(name, source, target, partner)
         at["side_in"][own_rows] = at["side_out"][own_rhs]
 
@@ -238,6 +257,7 @@
         convert_diag(1, low_cols // LANES)
         arrived("off0")
         convert_off(0, low_pairs)
+        load_tiles.wait()
         received("tiles", at["tiles_v"].at[1 - core])
         to_smem = pltpu.make_async_copy(at["tiles_v"], at["tiles_s"], local_sem.at[4])
         to_smem.start()
@@ -307,7 +327,7 @@
                 send(name, source, target.at[place], device)
                 return carry
 
-            lax.fori_loop(1, count, one, 0)
+            lax.fori_loop(0, count - 1, one, 0)
 
         def scatter(name, source, level):
             count = 2 ** (level - 1)
@@ -319,7 +339,7 @@
                 send(name, source.at[index], target.at[place], device)
                 return carry
 
-            lax.fori_loop(1, count, one, 0)
+            lax.fori_loop(0, count - 1, one, 0)
 
         def await_all(name, level):
             count = 2 ** (level - 1)
@@ -392,7 +412,7 @@
                 send(name, at[name + "_out"].at[index], at[name + "_in"].at[own_rhs], device)
                 return carry
 
-            lax.fori_loop(1, slots, one, 0)
+            lax.fori_loop(0, slots - 1, one, 0)
             at[name + "_in"][own_rhs] = at[name + "_out"][own_rows]
 
         def unpack(name, target):
@@ -464,22 +484,21 @@
         side = jnp.transpose(right_side, (0, 2, 1))
         off = jnp.transpose(off_diag, (0, 2, 1))
         tiles = jnp.transpose(tile_rows[:, :, 0], (1, 0))
-        tiles = jnp.pad(tiles, ((0, 8 - tiles.shape[0]), (0, LANES - pairs)))
         plan, moves = scratch_plan(levels, pairs, rows, cols, group, slots)
         vmem = pl.BlockSpec(memory_space=pltpu.VMEM)
-        anywhere = pl.BlockSpec(memory_space=pl.ANY)
+        hbm = pl.BlockSpec(memory_space=pltpu.HBM)
         out = jax.ShapeDtypeStruct(side.shape, jnp.float32)
         forward, backward = pl.pallas_call(
             make_kernel(levels, list(plan), moves, rows, cols, group, grid),
             out_shape=(out, out),
-            in_specs=[vmem, anywhere, anywhere, vmem],
+            in_specs=[hbm, hbm, hbm, hbm],
             out_specs=(vmem, vmem),
             scratch_shapes=list(plan.values()),
             compiler_params=pltpu.CompilerParams(
                 collective_id=0, has_side_effects=True, vmem_limit_bytes=48 * 2**20
             ),
             name="tree_solve",
-        )(side, diag_inv, off, tiles)
+        )(*(pltpu.with_memory_space_constraint(part, pltpu.HBM) for part in (side, diag_inv, off, tiles)))
         return jnp.transpose(forward, (0, 2, 1)), jnp.transpose(backward, (0, 2, 1))
 
     in_specs = (

time: 139 us -> 127 us (0.914)
  Pallas kernels: 132 us -> 125 us
  local copies, waits for them, and re-layouts: 5.68 us -> 1.25 us
    pallas_call x1, Pallas kernels: 132 us -> 125 us  [local(): pl.pallas_call(make_kernel(levels, list(plan), moves, rows, cols, group,...]
    unnamed x8 -> x2, local copies, waits for them, and re-layouts: 4.99 us -> 1.25 us
where the time goes in v2:
time: 127 us
  Pallas kernels  125 us (98%)
    pallas_call x1, Pallas kernels, local(): pl.pallas_call(make_kernel(levels, list(plan), moves, rows, cols, group,...  125 us

profile of v2, /device:TPU:1, one launch (start us, length us, event | category | flops | bytes accessed | tf_op | source)
XLA Modules:
  0.0 126.8 jit_solution(12574299748702785746)
XLA Ops:
  0.6 124.9 %tree_solve.1 = (f32[7,8,256]{2,1,0:T(8,128)S(1)}, f32[7,8,256]{2,1,0:T(8,128)S(1)}) custom-call(f32[7,8,256]{2,1,0:T(8,128)} %bitcast.10, f32[64,8128]{1,0:T(8,128)} %diag_hbm.1, f32[21,64,256]{2,1,0:T(8,128)} %bitcast.9, s32[2,21]{1,0:T(2,128)} %bitcast.11), custom_call_target="tpu_custom_call" | custom-call | tf_op jit(solution)/shard_map/tree_solve/pallas_call | solution.py:491
  125.5 0.6 copy.8
  126.2 0.6 copy.9

commit v3 on v2

v3 whole, which is shorter than its diff:
```python
import types

import jax
import jax.numpy as jnp
from jax import lax
from jax.experimental import pallas as pl
from jax.experimental.pallas import tpu as pltpu
from jax.sharding import PartitionSpec as P

MESH = pl.DeviceIdType.MESH
LANES = 128
ONE_STEP = 3
MIX_TOP = 5
NN = (((1,), (0,)), ((), ()))
NT = (((1,), (1,)), ((), ()))


def pair_slot(source, ancestor):
    return ancestor * (ancestor - 1) // 2 + source


def outward(place, size):
    away = (place + 1) // 2
    return lax.rem(size // 2 + away * (1 - 2 * lax.rem(place, 2)) + size, size)


def split(value):
    high = value.astype(jnp.bfloat16)
    low = (value - high.astype(jnp.float32)).astype(jnp.bfloat16)
    return high, low


def product(value, high, low, dims):
    rows = value.shape[0]
    value_high, value_low = split(value)
    both = lax.dot_general(
        jnp.concatenate([value_high, value_low], axis=0), high, dims, preferred_element_type=jnp.float32
    )
    rest = lax.dot_general(value_high, low, dims, preferred_element_type=jnp.float32)
    return both[:rows] + both[rows:] + rest


def scratch_plan(levels, pairs, rows, cols, group, slots):
    f32, bf16 = jnp.float32, jnp.bfloat16
    tile = (group, LANES)
    plan = {
        ("diag32", 0): pltpu.VMEM((2, rows, cols), f32),
        ("off32", 0): pltpu.VMEM((pairs, 2 * rows, 2 * LANES), f32),
        ("diag_high", 0): pltpu.VMEM((2 * rows, rows * 2**levels), bf16),
        ("diag_low", 0): pltpu.VMEM((2 * rows, rows * 2**levels), bf16),
        ("off_high", 0): pltpu.VMEM((pairs, 2 * rows, 2 * LANES), bf16),
        ("off_low", 0): pltpu.VMEM((pairs, 2 * rows, 2 * LANES), bf16),
        ("tiles_v", 0): pltpu.VMEM((2, 2, pairs), jnp.int32),
        ("tiles_s", 0): pltpu.SMEM((2, 2, pairs), jnp.int32),
    }
    plan["side32", 0] = pltpu.VMEM((levels, rows // (slots // 2), slots * group), f32)
    for name in ("side", "fwd", "sol"):
        plan[name + "_out", 0] = pltpu.VMEM((slots,) + tile, f32)
        plan[name + "_in", 0] = pltpu.VMEM((slots,) + tile, f32)
    for name in ("b", "y", "w", "x"):
        plan[name, 0] = pltpu.VMEM((levels,) + tile, f32)
    moves = ["side", "fwd", "sol", "diag0", "diag1", "off0", "off1", "tiles", "ptiles"]
    plan["ptiles_v", 0] = pltpu.VMEM((2 ** (MIX_TOP - 1), 2, pairs), jnp.int32)
    plan["ptiles_s", 0] = pltpu.SMEM((2 ** (MIX_TOP - 1), 2, pairs), jnp.int32)
    for level in range(1, levels):
        count = 2 ** (level - 1)
        plan["acc", level] = pltpu.VMEM((count,) + tile, f32)
        plan["full", level] = pltpu.VMEM((count,) + tile, f32)
        if level < 2:
            continue
        plan["part", level] = pltpu.VMEM((count,) + tile, f32)
        if level <= ONE_STEP:
            plan["up", level] = pltpu.VMEM((count, count) + tile, f32)
            plan["down", level] = pltpu.VMEM((count, count) + tile, f32)
            moves += [("up", level), ("down", level)]
        else:
            plan["up", level] = pltpu.VMEM((count,) + tile, f32)
            plan["down", level] = pltpu.VMEM((count,) + tile, f32)
            plan["sum", level] = pltpu.VMEM((count,) + tile, f32)
            moves += [("up", level), ("down", level), ("sum", level), ("full", level)]
            if level > MIX_TOP:
                continue
            plan["mid", level] = pltpu.VMEM((count,) + tile, f32)
            plan["mpart", level] = pltpu.VMEM((count,) + tile, f32)
            plan["lrow", level] = pltpu.VMEM((count, 2 * rows // slots, 2 * LANES), f32)
            plan["mix", level] = pltpu.VMEM((count, slots, 2 * rows // slots, LANES), f32)
            plan["block_high", level] = pltpu.VMEM((count, LANES, LANES), bf16)
            plan["block_low", level] = pltpu.VMEM((count, LANES, LANES), bf16)
            plan["mix_high", level] = pltpu.VMEM((count * LANES, LANES), bf16)
            plan["mix_low", level] = pltpu.VMEM((count * LANES, LANES), bf16)
            moves += [("mid", level), ("lrow", level), ("mix", level), ("swap", level)]
            if level == MIX_TOP:
                plan["new", level] = pltpu.VMEM((count,) + tile, f32)
                moves.append(("new", level))
    plan["send_sem", 0] = pltpu.SemaphoreType.DMA((len(moves),))
    plan["recv_sem", 0] = pltpu.SemaphoreType.DMA((len(moves),))
    plan["local_sem", 0] = pltpu.SemaphoreType.DMA((8,))
    return plan, moves


def make_kernel(levels, names, moves, rows, cols, group, grid):
    chunk = rows // grid
    slots = 2 * grid
    top = levels - 1
    chips = 2 ** (top - 1)
    low_cols = 1024
    low_pairs = 6
    ring = min(8, chips)

    def kernel(side_hbm, diag_hbm, off_hbm, tile_hbm, fwd_ref, sol_ref, *scratch):
        table = dict(zip(names, scratch))
        at = types.SimpleNamespace()
        for (name, level), ref in table.items():
            if level:
                vars(at).setdefault(name, {})[level] = ref
            else:
                vars(at)[name] = ref
        send_sem, recv_sem, local_sem = at.send_sem, at.recv_sem, at.local_sem
        slot_of = {name: place for place, name in enumerate(moves)}
        leaf, z = lax.axis_index("leaf"), lax.axis_index("grid")
        core = lax.rem(leaf, 2)
        chip = leaf // 2
        lane = lax.broadcasted_iota(jnp.int32, (group, LANES), 1)
        lane_block = lane // chunk
        left_half = lane < rows
        own_rhs = 2 * z + core
        own_rows = core * grid + z

        def column_device(step):
            their_z = lax.rem(z + outward(step // 2, grid), grid)
            their_core = lax.rem(core + 1 + lax.rem(step, 2), 2)
            return their_core, their_z, (2 * chip + their_core, their_z)

        def column_peer(step):
            their_core, their_z, device = column_device(step)
            return 2 * their_z + their_core, device

        def row_peer(step):
            their_core, their_z, device = column_device(step)
            return their_core * grid + their_z, device

        def plane_peer(count, step):
            place = lax.rem(chip, count)
            if count < ring:
                index = lax.rem(place + outward(step, count), count)
            else:
                lines = count // ring
                line = lax.rem(place // ring + outward(lax.rem(step, lines), lines), lines)
                index = line * ring + lax.rem(place + outward(step // lines, ring), ring)
            return index, (2 * (chip - place + index) + core, z)

        def send(name, source, target, device):
            pltpu.make_async_remote_copy(
                src_ref=source,
                dst_ref=target,
                send_sem=send_sem.at[slot_of[name]],
                recv_sem=recv_sem.at[slot_of[name]],
                device_id=device,
                device_id_type=MESH,
            ).start()

        def await_bytes(view, sem):
            pltpu.make_async_copy(view, view, sem).wait()

        sent = []

        def received(name, view):
            await_bytes(view, recv_sem.at[slot_of[name]])
            sent.append((name, view))

        diag32, off32 = at.diag32, at.off32
        low = pl.ds(0, low_cols)
        high = pl.ds(low_cols, cols - low_cols)
        mine = pl.ds(pl.multiple_of(core * rows, rows), rows)
        pairs = off_hbm.shape[0]
        low_p, high_p = pl.ds(0, low_pairs), pl.ds(low_pairs, pairs - low_pairs)
        load_side = pltpu.make_async_copy(side_hbm, at.side32, local_sem.at[5])
        load_side.start()
        load_tiles = pltpu.make_async_copy(tile_hbm, at.tiles_v.at[core], local_sem.at[6])
        load_tiles.start()
        parts = [
            ("diag0", diag_hbm.at[:, low], diag32.at[core, :, low]),
            ("off0", off_hbm.at[low_p], off32.at[low_p, mine, :]),
            ("off1", off_hbm.at[high_p], off32.at[high_p, mine, :]),
            ("diag1", diag_hbm.at[:, high], diag32.at[core, :, high]),
        ]
        own_copies = {}
        for place, (name, source, target) in enumerate(parts):
            own_copies[name] = pltpu.make_async_copy(source, target, local_sem.at[place])
            own_copies[name].start()

        barrier = pltpu.get_barrier_semaphore()

        def greet_column(step, carry):
            _, device = column_peer(step)
            pl.semaphore_signal(barrier, inc=1, device_id=device, device_id_type=MESH)
            return carry

        def greet_plane(step, carry):
            _, device = plane_peer(chips, step)
            pl.semaphore_signal(barrier, inc=1, device_id=device, device_id_type=MESH)
            return carry

        lax.fori_loop(0, slots - 1, greet_column, 0)
        lax.fori_loop(0, chips - 1, greet_plane, 0)

        used = levels * chunk
        load_side.wait()
        side = at.side32[...].reshape(used, slots * group)
        side = jnp.concatenate([side, jnp.zeros((LANES - used, slots * group), jnp.float32)], axis=0)
        at.side_out[...] = side.T.reshape(slots, group, LANES)
        for level in range(1, levels):
            at.acc[level][...] = jnp.zeros_like(at.acc[level])
        at.w[...] = jnp.zeros_like(at.w)

        pl.semaphore_wait(barrier, slots - 1 + chips - 1)

        def send_side(step, carry):
            index, device = column_peer(step)
            send("side", at.side_out.at[index], at.side_in.at[own_rows], device)
            return carry

        partner = (2 * chip + 1 - core, z)
        send("tiles", tile_hbm, at.tiles_v.at[core], partner)
        lax.fori_loop(0, slots - 1, send_side, 0)
        for name, source, target in parts:
            send(name, source, target, partner)
        load_tiles.wait()
        own_copies["off1"].wait()
        group_chips = 2 ** (MIX_TOP - 1)
        in_group = lax.rem(chip, group_chips)
        at.ptiles_v[in_group] = at.tiles_v[core]

        def send_tiles(step, carry):
            _, device = plane_peer(group_chips, step)
            send("ptiles", at.tiles_v.at[core], at.ptiles_v.at[in_group], device)
            return carry

        lax.fori_loop(0, group_chips - 1, send_tiles, 0)
        share = pl.ds(pl.multiple_of(core * rows + z * chunk, chunk), chunk)

        def send_rows(level):
            count = 2 ** (level - 1)
            place = lax.rem(chip, count)
            rows_of = at.lrow[level]
            p = pair_slot(level - 1, level)
            rows_of[place] = off32[p, share, :]

            def one(step, carry):
                _, device = plane_peer(count, step)
                send(("lrow", level), off32.at[p, share, :], rows_of.at[place], device)
                return carry

            lax.fori_loop(0, count - 1, one, 0)

        for level in range(MIX_TOP, ONE_STEP, -1):
            send_rows(level)
        at.side_in[own_rows] = at.side_out[own_rhs]

        other = pl.ds(pl.multiple_of((1 - core) * rows, rows), rows)
        theirs = {
            "diag0": diag32.at[1 - core, :, low],
            "off0": off32.at[low_p, other, :],
            "off1": off32.at[high_p, other, :],
            "diag1": diag32.at[1 - core, :, high],
        }

        def arrived(name):
            if name != "off1":
                own_copies[name].wait()
            received(name, theirs[name])

        def put_diag(half, place, value):
            value_high, value_low = split(value)
            spot = pl.ds(half * rows, rows)
            at.diag_high[spot, place] = value_high
            at.diag_low[spot, place] = value_low

        wide_lane = lax.broadcasted_iota(jnp.int32, (rows, LANES), 1)

        def convert_diag(first, last):
            def block(j, carry):
                here = pl.ds(pl.multiple_of(j * LANES, LANES), LANES)
                before = pl.ds(pl.multiple_of((j - 1) * LANES, LANES), LANES)
                for half in range(2):
                    mixed = jnp.where(wide_lane < rows, diag32[half, :, here], diag32[half, :, before])
                    put_diag(half, here, pltpu.roll(mixed, rows, 1))
                return carry

            lax.fori_loop(first, last, block, 0)

        def copy_blocks(level):
            start = rows * 2**level

            def block(j, carry):
                here = pl.ds(pl.multiple_of(start + j * LANES, LANES), LANES)
                at.block_high[level][j] = at.diag_high[:, here]
                at.block_low[level][j] = at.diag_low[:, here]
                return carry

            lax.fori_loop(0, 2 ** (level - 1), block, 0)

        def convert_last_diag():
            j = cols // LANES
            for half in range(2):
                tail = diag32[half, :, j * LANES : cols]
                tail = jnp.concatenate([tail, jnp.zeros((rows, LANES - rows), jnp.float32)], axis=1)
                mixed = jnp.where(wide_lane < rows, tail, diag32[half, :, (j - 1) * LANES : j * LANES])
                put_diag(half, pl.ds(j * LANES, LANES), pltpu.roll(mixed, rows, 1))

        def convert_off(first, last):
            def block(p, carry):
                value_high, value_low = split(off32[p])
                at.off_high[p] = value_high
                at.off_low[p] = value_low
                return carry

            lax.fori_loop(first, last, block, 0)

        arrived("diag0")
        for half in range(2):
            first = jnp.where(wide_lane < rows, diag32[half, :, 0:LANES], 0.0)
            put_diag(half, pl.ds(0, LANES), first if half == 0 else pltpu.roll(first, rows, 1))
        convert_diag(1, low_cols // LANES)
        arrived("off0")
        convert_off(0, low_pairs)
        received("tiles", at.tiles_v.at[1 - core])
        to_smem = pltpu.make_async_copy(at.tiles_v, at.tiles_s, local_sem.at[4])
        to_smem.start()
        to_smem.wait()
        tiles = at.tiles_s

        received("side", at.side_in.at[pl.ds(0, slots - 1)])
        turned = []
        for s in range(slots):
            value = at.side_in[s]
            turned.append(pltpu.roll(value, s * chunk, 1) if s else value)
        for level in range(levels):
            value = turned[0]
            for s in range(1, slots):
                value = jnp.where(lane_block == (s + level) % slots, turned[s], value)
            at.b[level] = pltpu.roll(value, LANES - level * chunk, 1) if level else value

        def diag_block(level):
            if level == 0:
                place = pl.ds(0, LANES)
            else:
                place = pl.ds(rows * 2**level, rows * 2**level)
            return at.diag_high[:, place], at.diag_low[:, place]

        def contribute(source, level):
            p = pair_slot(source, level)
            known = at.y[source]
            stacked = jnp.concatenate([jnp.where(left_half, known, 0.0), jnp.where(left_half, 0.0, known)], axis=0)
            out = product(stacked, at.off_high[p], at.off_low[p], NN)
            pieces = []
            for half in range(2):
                for t in range(2):
                    piece = out[half * group : (half + 1) * group, t * LANES : (t + 1) * LANES]
                    pieces.append((piece, tiles[half, t, p]))
            acc = at.acc[level]
            count = 2 ** (level - 1)

            def add(target, carry):
                value = acc[target]
                for piece, number in pieces:
                    value = value - piece * (number == target).astype(jnp.float32)
                acc[target] = value
                return carry

            if count <= 4:
                for target in range(count):
                    add(target, 0)
            else:
                lax.fori_loop(0, count, add, 0)

        def gather_known(ancestor, level):
            p = pair_slot(level, ancestor)
            full = at.full[ancestor]
            halves = []
            for half in range(2):
                halves.append(jnp.concatenate([full[tiles[half, t, p]] for t in range(2)], axis=1))
            out = product(jnp.concatenate(halves, axis=0), at.off_high[p], at.off_low[p], NT)
            at.w[level] += jnp.where(left_half, out[:group], out[group:])

        def broadcast(name, source, level):
            count = 2 ** (level - 1)
            place = lax.rem(chip, count)
            target = table[name]

            def one(step, carry):
                _, device = plane_peer(count, step)
                send(name, source, target.at[place], device)
                return carry

            lax.fori_loop(0, count - 1, one, 0)

        def scatter(name, source, level):
            count = 2 ** (level - 1)
            place = lax.rem(chip, count)
            target = table[name]

            def one(step, carry):
                index, device = plane_peer(count, step)
                send(name, source.at[index], target.at[place], device)
                return carry

            lax.fori_loop(0, count - 1, one, 0)

        def await_all(name, level):
            count = 2 ** (level - 1)
            received(name, table[name].at[pl.ds(0, count - 1)])

        def total(ref, count):
            value = ref[0]
            for place in range(1, count):
                value = value + ref[place]
            return value

        def build_mix(level):
            count = 2 ** (level - 1)
            first_chip = in_group - lax.rem(chip, count)
            p = pair_slot(level - 1, level)
            rows_of, mix, numbers = at.lrow[level], at.mix[level], at.ptiles_s
            block_high, block_low = at.block_high[level], at.block_low[level]
            copy_blocks(level)

            def one(index, carry):
                value = rows_of[index]
                high_part = value.astype(jnp.bfloat16).astype(jnp.float32)
                both = jnp.concatenate([high_part, value - high_part], axis=0).astype(jnp.bfloat16)
                out = jnp.zeros((2 * chunk, LANES), jnp.float32)
                rest = jnp.zeros((2 * chunk, LANES), jnp.float32)
                for t in range(2):
                    number = numbers[first_chip + index, t, p]
                    piece = both[:, t * LANES : (t + 1) * LANES]
                    out += lax.dot_general(piece, block_high[number], NT, preferred_element_type=jnp.float32)
                    rest += lax.dot_general(piece, block_low[number], NT, preferred_element_type=jnp.float32)
                mix[index, own_rows] = out[:chunk] + out[chunk:] + rest[:chunk]
                return carry

            lax.fori_loop(0, count, one, 0)

            def give(step, carry):
                their_z = lax.rem(z + outward(step, grid), grid)
                part = mix.at[:, own_rows]
                send(("mix", level), part, part, (leaf, their_z))
                return carry

            lax.fori_loop(0, grid - 1, give, 0)

        def swap_mix(level):
            mix = at.mix[level]
            received(("mix", level), mix.at[:, pl.ds(0, grid - 1)])
            half = mix.at[:, pl.ds(core * grid, grid)]
            send(("swap", level), half, half, partner)

        def finish_mix(level):
            count = 2 ** (level - 1)
            mix = at.mix[level]
            received(("swap", level), mix.at[:, pl.ds((1 - core) * grid, grid)])

            def one(index, carry):
                value_high, value_low = split(mix[index].reshape(LANES, LANES))
                spot = pl.ds(pl.multiple_of(index * LANES, LANES), LANES)
                at.mix_high[level][spot, :] = value_high
                at.mix_low[level][spot, :] = value_low
                return carry

            lax.fori_loop(0, count, one, 0)

        at.y[0] = product(at.b[0], *diag_block(0), NT)
        contribute(0, 1)
        at.y[1] = product(at.b[1] + at.acc[1][0], *diag_block(1), NT)
        contribute(0, 2)
        def start_sums(level):
            count = 2 ** (level - 1)
            place = lax.rem(chip, count)
            acc, up = at.acc[level], at.up[level]
            if level <= ONE_STEP:
                acc[place] += at.b[level]
                broadcast(("up", level), acc, level)
                up[place] = acc[...]
            else:
                scatter(("up", level), acc, level)
                up[place] = acc[place]

        def spread_sum(level):
            count = 2 ** (level - 1)
            place = lax.rem(chip, count)
            await_all(("up", level), level)
            summed = at.sum[level]
            summed[place] = at.b[level] + total(at.up[level], count)
            broadcast(("sum", level), summed.at[place], level)

        def side_by_side(value, count):
            return jnp.concatenate([value[t] for t in range(count)], axis=1)

        def solve_level(level):
            count = 2 ** (level - 1)
            if level <= ONE_STEP:
                await_all(("up", level), level)
                whole = total(at.up[level], count)
            else:
                await_all(("sum", level), level)
                whole = at.sum[level][...]
            return product(side_by_side(whole, count), *diag_block(level), NT)

        contribute(1, 2)
        start_sums(2)
        contribute(0, 3)
        contribute(1, 3)
        arrived("off1")
        convert_off(low_pairs, pairs)
        at.y[2] = solve_level(2)
        contribute(2, 3)
        start_sums(3)
        for source in range(3):
            contribute(source, 4)
        arrived("diag1")
        convert_diag(low_cols // LANES, rows * 2 ** (MIX_TOP + 1) // LANES)
        received("ptiles", at.ptiles_v.at[pl.ds(0, group_chips - 1)])
        for upper in range(ONE_STEP + 1, MIX_TOP + 1):
            await_all(("lrow", upper), upper)
        numbers = pltpu.make_async_copy(at.ptiles_v, at.ptiles_s, local_sem.at[7])
        numbers.start()
        numbers.wait()
        build_mix(MIX_TOP)
        at.y[3] = solve_level(3)
        contribute(3, 4)
        start_sums(4)
        for source in range(4):
            contribute(source, MIX_TOP)
        start_sums(MIX_TOP)
        spread_sum(4)
        build_mix(4)
        spread_sum(MIX_TOP)
        at.y[4] = solve_level(4)
        count = 2 ** (MIX_TOP - 1)
        new = at.new[MIX_TOP]
        place = lax.rem(chip, count)
        new[place] = at.y[4]
        broadcast(("new", MIX_TOP), new.at[place], MIX_TOP)
        swap_mix(MIX_TOP)
        known = solve_level(MIX_TOP)
        for source in range(MIX_TOP):
            contribute(source, top)
        finish_mix(MIX_TOP)
        await_all(("new", MIX_TOP), MIX_TOP)
        at.y[MIX_TOP] = known - product(
            side_by_side(new[...], count), at.mix_high[MIX_TOP][...], at.mix_low[MIX_TOP][...], NN
        )
        contribute(MIX_TOP, top)
        start_sums(top)
        convert_diag(rows * 2**top // LANES, cols // LANES)
        convert_last_diag()
        spread_sum(top)
        swap_mix(4)
        finish_mix(4)
        at.y[top] = solve_level(top)

        def pack(values, name, outbox, inbox):
            turned = []
            for level in range(levels):
                value = values[level]
                turned.append(pltpu.roll(value, level * chunk, 1) if level else value)
            for s in range(slots):
                value = turned[0]
                for level in range(1, levels):
                    value = jnp.where(lane_block == (s + level) % slots, turned[level], value)
                outbox[s] = pltpu.roll(value, LANES - s * chunk, 1) if s else value

            def one(step, carry):
                index, device = row_peer(step)
                send(name, outbox.at[index], inbox.at[own_rhs], device)
                return carry

            lax.fori_loop(0, slots - 1, one, 0)
            inbox[own_rhs] = outbox[own_rows]

        def unpack(name, inbox, target):
            received(name, inbox.at[pl.ds(0, slots - 1)])
            value = inbox[...].reshape(slots * group, LANES).T
            for level in range(levels):
                target[level] = value[level * chunk : (level + 1) * chunk]

        def start_level(level):
            count = 2 ** (level - 1)
            place = lax.rem(chip, count)
            residue = at.y[level] - at.w[level]
            part, down = at.part[level], at.down[level]
            value = product(residue, *diag_block(level), NN)
            for t in range(count):
                part[t] = value[:, t * LANES : (t + 1) * LANES]
            if level <= ONE_STEP:
                broadcast(("down", level), part, level)
                down[place] = part[...]
                return
            if level > MIX_TOP:
                scatter(("down", level), part, level)
                down[place] = part[place]
                return
            mpart, mid = at.mpart[level], at.mid[level]
            value = product(residue, at.mix_high[level][...], at.mix_low[level][...], NT)
            for t in range(count):
                mpart[t] = value[:, t * LANES : (t + 1) * LANES]
            scatter(("mid", level), mpart, level)
            mid[place] = mpart[place]
            scatter(("down", level), part, level)
            down[place] = part[place]

        def spread_x(level):
            count = 2 ** (level - 1)
            place = lax.rem(chip, count)
            await_all(("down", level), level)
            value = total(at.down[level], count)
            at.x[level] = value
            at.full[level][place] = value
            broadcast(("full", level), at.full[level].at[place], level)

        def through_mix(level):
            await_all(("mid", level), level)
            at.w[level - 1] += total(at.mid[level], 2 ** (level - 1))

        def whole_x(level):
            count = 2 ** (level - 1)
            await_all(("down", level), level)
            at.full[level][...] = total(at.down[level], count)
            at.x[level] = at.full[level][lax.rem(chip, count)]

        start_level(top)
        pack(at.y, "fwd", at.fwd_out, at.fwd_in)
        spread_x(top)
        await_all(("full", top), top)
        gather_known(top, MIX_TOP)
        start_level(MIX_TOP)
        gather_known(top, MIX_TOP - 1)
        through_mix(MIX_TOP)
        start_level(ONE_STEP + 1)
        for below in range(ONE_STEP, -1, -1):
            gather_known(top, below)
        spread_x(MIX_TOP)
        through_mix(ONE_STEP + 1)
        await_all(("full", MIX_TOP), MIX_TOP)
        gather_known(MIX_TOP, ONE_STEP)
        start_level(ONE_STEP)
        spread_x(ONE_STEP + 1)
        for below in range(ONE_STEP - 1, -1, -1):
            gather_known(ONE_STEP + 2, below)
        unpack("fwd", at.fwd_in, fwd_ref)
        whole_x(ONE_STEP)
        await_all(("full", ONE_STEP + 1), ONE_STEP + 1)
        for below in range(ONE_STEP - 1, -1, -1):
            gather_known(ONE_STEP + 1, below)
        gather_known(ONE_STEP, ONE_STEP - 1)
        start_level(2)
        for below in (1, 0):
            gather_known(ONE_STEP, below)
        whole_x(2)
        gather_known(2, 1)
        value = product(at.y[1] - at.w[1], *diag_block(1), NN)
        at.x[1] = value
        at.full[1][0] = value
        gather_known(2, 0)
        gather_known(1, 0)
        at.x[0] = product(at.y[0] - at.w[0], *diag_block(0), NN)
        pack(at.x, "sol", at.sol_out, at.sol_in)
        unpack("sol", at.sol_in, sol_ref)
        for name, view in sent:
            await_bytes(view, send_sem.at[slot_of[name]])

    return kernel


def solution(mesh):
    grid = mesh.shape["grid"]

    def local(right_side, diag_inv, off_diag, tile_rows):
        levels, rhs, chunk = right_side.shape
        rows, cols = diag_inv.shape
        pairs = off_diag.shape[0]
        slots = 2 * grid
        group = rhs // slots
        side = jnp.transpose(right_side, (0, 2, 1))
        off = jnp.transpose(off_diag, (0, 2, 1))
        tiles = jnp.transpose(tile_rows[:, :, 0], (1, 0))
        plan, moves = scratch_plan(levels, pairs, rows, cols, group, slots)
        vmem = pl.BlockSpec(memory_space=pltpu.VMEM)
        hbm = pl.BlockSpec(memory_space=pltpu.HBM)
        out = jax.ShapeDtypeStruct(side.shape, jnp.float32)
        forward, backward = pl.pallas_call(
            make_kernel(levels, list(plan), moves, rows, cols, group, grid),
            out_shape=(out, out),
            in_specs=[hbm, hbm, hbm, hbm],
            out_specs=(vmem, vmem),
            scratch_shapes=list(plan.values()),
            compiler_params=pltpu.CompilerParams(
                collective_id=0, has_side_effects=True, vmem_limit_bytes=48 * 2**20
            ),
            name="tree_solve",
        )(*(pltpu.with_memory_space_constraint(part, pltpu.HBM) for part in (side, diag_inv, off, tiles)))
        return jnp.transpose(forward, (0, 2, 1)), jnp.transpose(backward, (0, 2, 1))

    in_specs = (
        P(None, None, ("leaf", "grid")),
        P("leaf", None),
        P(None, None, "leaf"),
        P(None, None, "leaf"),
    )
    out_specs = (P(None, None, ("leaf", "grid")), P(None, None, ("leaf", "grid")))
    return jax.shard_map(local, mesh=mesh, in_specs=in_specs, out_specs=out_specs, check_vma=False)
```

time: 127 us -> 118 us (0.929)
  Pallas kernels: 125 us -> 116 us
    pallas_call x1, Pallas kernels: 125 us -> 116 us  [local(): pl.pallas_call(make_kernel(levels, list(plan), moves, rows, cols, group,...]
where the time goes in v3:
time: 118 us
  Pallas kernels  116 us (98%)
  local copies, waits for them, and re-layouts  1.25 us (1%)
    pallas_call x1, Pallas kernels, local(): pl.pallas_call(make_kernel(levels, list(plan), moves, rows, cols, group,...  116 us

profile of v3, /device:TPU:1, one launch (start us, length us, event | category | flops | bytes accessed | tf_op | source)
XLA Modules:
  0.0 118.1 jit_solution(14596196753144154329)
XLA Ops:
  0.6 116.2 %tree_solve.1 = (f32[7,8,256]{2,1,0:T(8,128)S(1)}, f32[7,8,256]{2,1,0:T(8,128)S(1)}) custom-call(f32[7,8,256]{2,1,0:T(8,128)} %bitcast.10, f32[64,8128]{1,0:T(8,128)} %diag_hbm.1, f32[21,64,256]{2,1,0:T(8,128)} %bitcast.9, s32[2,21]{1,0:T(2,128)} %bitcast.11), custom_call_target="tpu_custom_call" | custom-call | tf_op jit(solution)/shard_map/tree_solve/pallas_call | solution.py:691
  116.8 0.6 copy.8
  117.5 0.6 copy.9

commit v4 on v3

--- a/solution.py
+++ b/solution.py
@@ -55,8 +55,8 @@
     }
     plan["side32", 0] = pltpu.VMEM((levels, rows // (slots // 2), slots * group), f32)
     for name in ("side", "fwd", "sol"):
-        plan[name + "_out", 0] = pltpu.VMEM((slots,) + tile, f32)
-        plan[name + "_in", 0] = pltpu.VMEM((slots,) + tile, f32)
+        plan[name + "_out", 0] = pltpu.VMEM((slots, group // 2, LANES), f32)
+        plan[name + "_in", 0] = pltpu.VMEM((slots, group // 2, LANES), f32)
     for name in ("b", "y", "w", "x"):
         plan[name, 0] = pltpu.VMEM((levels,) + tile, f32)
     moves = ["side", "fwd", "sol", "diag0", "diag1", "off0", "off1", "tiles", "ptiles"]
@@ -145,9 +145,21 @@
                 index = lax.rem(place + outward(step, count), count)
             else:
                 lines = count // ring
-                line = lax.rem(place // ring + outward(lax.rem(step, lines), lines), lines)
-                index = line * ring + lax.rem(place + outward(step // lines, ring), ring)
+                line = lax.rem(place // ring + outward(step // ring, lines), lines)
+                index = line * ring + lax.rem(place + ring + (1 - 2 * core) * outward(lax.rem(step, ring), ring), ring)
             return index, (2 * (chip - place + index) + core, z)
+
+        fold_rows = group // 2
+
+        def fold(value):
+            axis = value.ndim - 1
+            lanes = lax.broadcasted_iota(jnp.int32, value.shape[:-2] + (fold_rows, LANES), axis)
+            upper, lower = value[..., :fold_rows, :], value[..., fold_rows:, :]
+            return jnp.where(lanes < LANES // 2, upper, pltpu.roll(lower, LANES // 2, axis))
+
+        def unfold(value):
+            axis = value.ndim - 1
+            return jnp.concatenate([value, pltpu.roll(value, LANES // 2, axis)], axis=axis - 1)
 
         def send(name, source, target, device):
             pltpu.make_async_remote_copy(
@@ -201,14 +213,14 @@
             pl.semaphore_signal(barrier, inc=1, device_id=device, device_id_type=MESH)
             return carry
 
+        lax.fori_loop(0, chips - 1, greet_plane, 0)
         lax.fori_loop(0, slots - 1, greet_column, 0)
-        lax.fori_loop(0, chips - 1, greet_plane, 0)
 
         used = levels * chunk
         load_side.wait()
         side = at.side32[...].reshape(used, slots * group)
         side = jnp.concatenate([side, jnp.zeros((LANES - used, slots * group), jnp.float32)], axis=0)
-        at.side_out[...] = side.T.reshape(slots, group, LANES)
+        at.side_out[...] = fold(side.T.reshape(slots, group, LANES))
         for level in range(1, levels):
             at.acc[level][...] = jnp.zeros_like(at.acc[level])
         at.w[...] = jnp.zeros_like(at.w)
@@ -333,7 +345,7 @@
         received("side", at.side_in.at[pl.ds(0, slots - 1)])
         turned = []
         for s in range(slots):
-            value = at.side_in[s]
+            value = unfold(at.side_in[s])
             turned.append(pltpu.roll(value, s * chunk, 1) if s else value)
         for level in range(levels):
             value = turned[0]
@@ -568,7 +580,7 @@
                 value = turned[0]
                 for level in range(1, levels):
                     value = jnp.where(lane_block == (s + level) % slots, turned[level], value)
-                outbox[s] = pltpu.roll(value, LANES - s * chunk, 1) if s else value
+                outbox[s] = fold(pltpu.roll(value, LANES - s * chunk, 1) if s else value)
 
             def one(step, carry):
                 index, device = row_peer(step)
@@ -580,7 +592,7 @@
 
         def unpack(name, inbox, target):
             received(name, inbox.at[pl.ds(0, slots - 1)])
-            value = inbox[...].reshape(slots * group, LANES).T
+            value = unfold(inbox[...]).reshape(slots * group, LANES).T
             for level in range(levels):
                 target[level] = value[level * chunk : (level + 1) * chunk]
 
@@ -637,9 +649,9 @@
         gather_known(top, MIX_TOP - 1)
         through_mix(MIX_TOP)
         start_level(ONE_STEP + 1)
+        spread_x(MIX_TOP)
         for below in range(ONE_STEP, -1, -1):
             gather_known(top, below)
-        spread_x(MIX_TOP)
         through_mix(ONE_STEP + 1)
         await_all(("full", MIX_TOP), MIX_TOP)
         gather_known(MIX_TOP, ONE_STEP)
@@ -650,11 +662,11 @@
         unpack("fwd", at.fwd_in, fwd_ref)
         whole_x(ONE_STEP)
         await_all(("full", ONE_STEP + 1), ONE_STEP + 1)
-        for below in range(ONE_STEP - 1, -1, -1):
-            gather_known(ONE_STEP + 1, below)
-        gather_known(ONE_STEP, ONE_STEP - 1)
+        gather_known(ONE_STEP + 1, 2)
+        gather_known(ONE_STEP, 2)
         start_level(2)
         for below in (1, 0):
+            gather_known(ONE_STEP + 1, below)
             gather_known(ONE_STEP, below)
         whole_x(2)
         gather_known(2, 1)

time: 118 us -> 115 us (0.975)
  Pallas kernels: 116 us -> 113 us
    pallas_call x1, Pallas kernels: 116 us -> 113 us  [local(): pl.pallas_call(make_kernel(levels, list(plan), moves, rows, cols, group,...]
where the time goes in v4:
time: 115 us
  Pallas kernels  113 us (98%)
  local copies, waits for them, and re-layouts  1.25 us (1%)
    pallas_call x1, Pallas kernels, local(): pl.pallas_call(make_kernel(levels, list(plan), moves, rows, cols, group,...  113 us

profile of v4, /device:TPU:1, one launch (start us, length us, event | category | flops | bytes accessed | tf_op | source)
XLA Modules:
  0.0 114.9 jit_solution(9154070218804370841)
XLA Ops:
  0.6 113.0 %tree_solve.1 = (f32[7,8,256]{2,1,0:T(8,128)S(1)}, f32[7,8,256]{2,1,0:T(8,128)S(1)}) custom-call(f32[7,8,256]{2,1,0:T(8,128)} %bitcast.10, f32[64,8128]{1,0:T(8,128)} %diag_hbm.1, f32[21,64,256]{2,1,0:T(8,128)} %bitcast.9, s32[2,21]{1,0:T(2,128)} %bitcast.11), custom_call_target="tpu_custom_call" | custom-call | tf_op jit(solution)/shard_map/tree_solve/pallas_call | solution.py:703
  113.7 0.6 copy.8
  114.3 0.6 copy.9

commit v5 on v4

--- a/solution.py
+++ b/solution.py
@@ -127,7 +127,7 @@
         own_rows = core * grid + z
 
         def column_device(step):
-            their_z = lax.rem(z + outward(step // 2, grid), grid)
+            their_z = lax.rem(z + grid + (1 - 2 * core) * outward(step // 2, grid), grid)
             their_core = lax.rem(core + 1 + lax.rem(step, 2), 2)
             return their_core, their_z, (2 * chip + their_core, their_z)
 
@@ -454,7 +454,7 @@
             lax.fori_loop(0, count, one, 0)
 
             def give(step, carry):
-                their_z = lax.rem(z + outward(step, grid), grid)
+                their_z = lax.rem(z + grid + (1 - 2 * core) * outward(step, grid), grid)
                 part = mix.at[:, own_rows]
                 send(("mix", level), part, part, (leaf, their_z))
                 return carry

time: 115 us -> 115 us (level)
  no operation moved by 1% of the time
where the time goes in v5:
time: 115 us
  Pallas kernels  113 us (98%)
  local copies, waits for them, and re-layouts  1.25 us (1%)
    pallas_call x1, Pallas kernels, local(): pl.pallas_call(make_kernel(levels, list(plan), moves, rows, cols, group,...  113 us

profile of v5, /device:TPU:1, one launch (start us, length us, event | category | flops | bytes accessed | tf_op | source)
XLA Modules:
  0.0 115.3 jit_solution(13486511559883673662)
XLA Ops:
  0.6 113.4 %tree_solve.1 = (f32[7,8,256]{2,1,0:T(8,128)S(1)}, f32[7,8,256]{2,1,0:T(8,128)S(1)}) custom-call(f32[7,8,256]{2,1,0:T(8,128)} %bitcast.10, f32[64,8128]{1,0:T(8,128)} %diag_hbm.1, f32[21,64,256]{2,1,0:T(8,128)} %bitcast.9, s32[2,21]{1,0:T(2,128)} %bitcast.11), custom_call_target="tpu_custom_call" | custom-call | tf_op jit(solution)/shard_map/tree_solve/pallas_call | solution.py:703
  114.0 0.6 copy.8
  114.6 0.6 copy.9
